TPU v7x, 256 devices: a whole 4x4x8 slice. The times are simulated.
256 devices in a mesh: layer: 16 (over x, y), dp: 4 (over z_lo, core), tensor: 4 (over z_hi).
Axes of the slice: x: 4, y: 4, z: 8 (z_hi: 4, z_lo: 2; z = z_hi * 2 + z_lo), core: 2. Of those that a mesh axis runs over, the one named last changes fastest.
Arguments:
- hidden: bfloat16 [2, 16384, 8192], P(None, ('layer', 'dp'), 'tensor'), may hold values from -60 to 60
- queries: bfloat16 [2, 16384, 4096], P(None, ('layer', 'dp'), 'tensor'), may hold values from -70 to 70
- cotangent: bfloat16 [2, 16384, 4096], P(None, ('layer', 'dp'), 'tensor'), may hold values from -6 to 6
- slabs: bfloat16 [2, 8192, 1024], P(None, 'layer', 'tensor'), may hold values from -0.0625 to 0.0625
Outputs:
- attended: bfloat16 [2, 16384, 4096], P(None, ('layer', 'dp'), 'tensor')
- query_grads: bfloat16 [2, 16384, 4096], P(None, ('layer', 'dp'), 'tensor')
- hidden_grads: bfloat16 [2, 16384, 8192], P(None, ('layer', 'dp'), 'tensor')
- slab_grads: float32 [2, 8192, 1024], P(None, 'layer', 'tensor')
All inputs are finite; a program needn't handle non-finite values.
Results may differ from a plain program's by a relative error of at most 0.025.
The roundings to bfloat16 on the way count: a program that leaves them out, or rounds other values in their place, can miss the bound.
Values may be sent and summed in bfloat16 or wider, within the bound.
No kernel may reach another device: no remote copies, remote signals or barrier semaphores. Data moves between devices by JAX's collectives and lax.ppermute only.
A program may use at most 128 MiB of HBM per device.

v0:
```python
import jax
import jax.numpy as jnp
from jax import lax
from jax.sharding import PartitionSpec as P

D = 8192
HD = 128
GROUP = 8
SEQ_LEN = 256


EPSILON = 1e-05


def attend(query_rows, key_rows, value_rows):
    scores = jnp.einsum(
        "slhge,smhe->shglm", query_rows.astype(jnp.float32), key_rows.astype(jnp.float32)
    )
    scores = scores * query_rows.shape[-1] ** (-0.5)
    length = query_rows.shape[1]
    position = jnp.arange(length)
    causal = position[:, None] >= position[None, :]
    scores = jnp.where(causal, scores, -1e30)
    highest = jnp.max(scores, axis=-1, keepdims=True)
    weights = jnp.exp(scores - highest)
    weights = (weights / jnp.sum(weights, axis=-1, keepdims=True)).astype(jnp.bfloat16)
    mixed_rows = jnp.einsum(
        "shglm,smhe->slhge", weights.astype(jnp.float32), value_rows.astype(jnp.float32)
    )
    return mixed_rows.astype(jnp.bfloat16)


def normalize(state_rows):
    floats = state_rows.astype(jnp.float32)
    inverse = lax.rsqrt(jnp.mean(floats * floats, axis=-1, keepdims=True) + EPSILON)
    return (floats * inverse, inverse)


def fetch_slab(owned_rows):
    return lax.all_gather(owned_rows, "layer", axis=0, tiled=True)


def shards(hidden, queries, cotangent, slabs):
    token_count = hidden.shape[1]
    part_width = hidden.shape[2]
    seq_count = token_count // SEQ_LEN
    tensor_index = lax.axis_index("tensor")
    owned_count = slabs.shape[1]
    attended_list = []
    query_list = []
    hidden_list = []
    slab_list = []
    for depth in range(2):
        layer_slab = fetch_slab(slabs[depth])
        full_rows = lax.all_gather(hidden[depth], "tensor", axis=1, tiled=True)
        scaled, inverse = normalize(full_rows)
        normed = scaled.astype(jnp.bfloat16)
        projected = jnp.dot(normed, layer_slab, preferred_element_type=jnp.float32).astype(
            jnp.bfloat16
        )
        key_rows = projected[:, :HD].reshape(seq_count, SEQ_LEN, 1, HD)
        value_rows = projected[:, HD:].reshape(seq_count, SEQ_LEN, 1, HD)
        query_rows = queries[depth].reshape(seq_count, SEQ_LEN, 1, GROUP, HD)
        output, pullback = jax.vjp(attend, query_rows, key_rows, value_rows)
        query_grad, key_grad, value_grad = pullback(
            cotangent[depth].reshape(seq_count, SEQ_LEN, 1, GROUP, HD)
        )
        joined = jnp.concatenate(
            [key_grad.reshape(token_count, HD), value_grad.reshape(token_count, HD)], axis=1
        )
        spread_term = lax.dot_general(
            joined, layer_slab, (((1,), (1,)), ((), ())), preferred_element_type=jnp.float32
        )
        spread = lax.psum_scatter(
            spread_term.astype(jnp.bfloat16), "tensor", scatter_dimension=1, tiled=True
        ).astype(jnp.float32)
        local_scaled = lax.dynamic_slice_in_dim(scaled, tensor_index * part_width, part_width, 1)
        products = lax.psum(jnp.sum(spread * local_scaled, axis=-1, keepdims=True), "tensor") / D
        input_grad = (inverse * (spread - local_scaled * products)).astype(jnp.bfloat16)

        def slab_term(first_row, row_span, normed=normed, joined=joined):
            return lax.dot_general(
                normed, joined, (((0,), (0,)), ((), ())), preferred_element_type=jnp.float32
            )

        owned_grad = lax.psum_scatter(
            slab_term(jnp.int32(0), owned_count * lax.axis_size("layer")).astype(jnp.bfloat16),
            "layer",
            scatter_dimension=0,
            tiled=True,
        )
        slab_grad = lax.psum(owned_grad, "dp").astype(jnp.float32)
        attended_list.append(output.reshape(token_count, GROUP * HD))
        query_list.append(query_grad.reshape(token_count, GROUP * HD))
        hidden_list.append(input_grad)
        slab_list.append(slab_grad)
    return (
        jnp.stack(attended_list),
        jnp.stack(query_list),
        jnp.stack(hidden_list),
        jnp.stack(slab_list),
    )


def solution(mesh):
    in_specs = (
        P(None, ("layer", "dp"), "tensor"),
        P(None, ("layer", "dp"), "tensor"),
        P(None, ("layer", "dp"), "tensor"),
        P(None, "layer", "tensor"),
    )
    out_specs = (
        P(None, ("layer", "dp"), "tensor"),
        P(None, ("layer", "dp"), "tensor"),
        P(None, ("layer", "dp"), "tensor"),
        P(None, "layer", "tensor"),
    )
    return jax.shard_map(shards, mesh=mesh, in_specs=in_specs, out_specs=out_specs, check_vma=False)
```

profile of v0, /device:TPU:71, one launch (start us, length us, event | category | flops | bytes accessed | tf_op | source)
XLA Modules:
  0.0 714.6 jit_solution(15656241773818859510)
XLA Ops:
  7.2 3.1 fusion.110
  15.5 69.9 %all-gather.13.cloned.1.call-done = bf16[1,256,8192]{2,1,0:T(8,128)(2,1)} async-done(((bf16[1,256,2048]{2,1,0:T(8,128)(2,1)}), bf16[1,256,8192]{2,1,0:T(8,128)(2,1)}) %all-gather.13.cloned.1.call-update) | async-done | bytes 4194320 | tf_op jit(solution)/shard_map/all_gather | solution.py:55
  85.4 3.1 fusion.1
  88.6 83.9 %all-gather.9.cloned.1.call-done = bf16[1,256,8192]{2,1,0:T(8,128)(2,1)} async-done(((bf16[1,256,2048]{2,1,0:T(8,128)(2,1)}), bf16[1,256,8192]{2,1,0:T(8,128)(2,1)}) %all-gather.9.cloned.1.call-update) | async-done | bytes 4194320 | tf_op jit(solution)/shard_map/all_gather | solution.py:55
  175.5 68.3 %all-gather.15.cloned.1.call-done = bf16[1,8192,256]{2,1,0:T(8,128)(2,1)} async-done(((bf16[1,512,256]{2,1,0:T(8,128)(2,1)}), bf16[1,8192,256]{2,1,0:T(8,128)(2,1)}) %all-gather.15.cloned.1.call-update) | async-done | bytes 4194320 | tf_op jit(solution)/shard_map/all_gather | solution.py:40
  243.8 4.8 fusion.51
  251.0 52.0 %all-gather.11.cloned.1.call-done = bf16[1,8192,256]{2,1,0:T(8,128)(2,1)} async-done(((bf16[1,512,256]{2,1,0:T(8,128)(2,1)}), bf16[1,8192,256]{2,1,0:T(8,128)(2,1)}) %all-gather.11.cloned.1.call-update) | async-done | bytes 4194320 | tf_op jit(solution)/shard_map/all_gather | solution.py:40
  303.0 4.8 fusion.46
  310.4 3.2 fusion.106
  317.4 3.3 convolution_convert_fusion.2
  322.5 3.5 fusion.67
  326.6 3.3 convolution_convert_fusion.3
  330.0 6.0 convolution_convert_fusion.1
  336.6 5.9 convolution_convert_fusion
  342.8 6.7 convert_multiply_fusion
  349.5 4.3 convert_multiply_fusion.2
  357.0 3.4 fusion.43
  365.1 3.4 fusion.40
  371.9 33.0 %reduce-scatter.7.cloned.1.call-done = bf16[256,2048]{1,0:T(8,128)(2,1)} async-done(((bf16[256,8192]{1,0:T(8,128)(2,1)}), bf16[256,2048]{1,0:T(8,128)(2,1)}) %reduce-scatter.7.cloned.1.call-update) | async-done | bytes 1048592 | tf_op jit(solution)/shard_map/reduce_scatter | solution.py:74
  407.1 81.7 %reduce-scatter.5.cloned.1.call-done = bf16[256,2048]{1,0:T(8,128)(2,1)} async-done(((bf16[256,8192]{1,0:T(8,128)(2,1)}), bf16[256,2048]{1,0:T(8,128)(2,1)}) %reduce-scatter.5.cloned.1.call-update) | async-done | bytes 1048592 | tf_op jit(solution)/shard_map/reduce_scatter | solution.py:74
  491.1 8.7 %all-reduce = (f32[256,1]{0,1:T(1,128)S(1)}, f32[256,1]{0,1:T(1,128)S(1)}) all-reduce(f32[256,1]{0,1:T(1,128)S(1)} %bitcast.236, f32[256,1]{0,1:T(1,128)S(1)} %bitcast.237), channel_id=1, replica_groups=mesh['layer'=16,'dp'=4,'tensor'=4] {'tensor'}, use_global_device_ids=true, to_apply=%region_17.18 | all-reduce | flops 512 | bytes 4096 | tf_op jit(solution)/shard_map/psum | solution.py:78
  499.8 73.1 %reduce-scatter.9.cloned.1.call-done = bf16[512,256]{1,0:T(8,128)(2,1)} async-done(((bf16[8192,256]{1,0:T(8,128)(2,1)}), bf16[512,256]{1,0:T(8,128)(2,1)}) %reduce-scatter.9.cloned.1.call-update) | async-done | bytes 262160 | tf_op jit(solution)/shard_map/reduce_scatter | solution.py:86
  572.9 86.1 %reduce-scatter.11.cloned.1.call-done = bf16[512,256]{1,0:T(8,128)(2,1)} async-done(((bf16[8192,256]{1,0:T(8,128)(2,1)}), bf16[512,256]{1,0:T(8,128)(2,1)}) %reduce-scatter.11.cloned.1.call-update) | async-done | bytes 262160 | tf_op jit(solution)/shard_map/reduce_scatter | solution.py:86
  664.7 41.3 %all-reduce.4.cloned.1.call-done = (bf16[1,512,256]{2,1,0:T(8,128)(2,1)}, bf16[1,512,256]{2,1,0:T(8,128)(2,1)}) async-done(((bf16[1,512,256]{2,1,0:T(8,128)(2,1)}, bf16[1,512,256]{2,1,0:T(8,128)(2,1)}), (bf16[1,512,256]{2,1,0:T(8,128)(2,1)}, bf16[1,512,256]{2,1,0:T(8,128)(2,1)})) %all-reduce.4.cloned.1.call-update) | async-done | bytes 524304 | tf_op jit(solution)/shard_map/psum | solution.py:92
  (146 shorter events, 43.4 us)
Async XLA Ops:
  7.2 78.3 %all-gather.13.cloned.1.call-start = ((), (), s32[]{:S(2)}) async-start(), calls=%async_computation.10 | async-start | bytes 5242880 | tf_op jit(solution)/shard_map/all_gather | solution.py:55
  10.3 162.1 %all-gather.9.cloned.1.call-start = ((), (), s32[]{:S(2)}) async-start(), calls=%async_computation.8 | async-start | bytes 5242880 | tf_op jit(solution)/shard_map/all_gather | solution.py:55
  11.1 232.7 %all-gather.15.cloned.1.call-start = ((), (), s32[]{:S(2)}) async-start(), calls=%async_computation.11 | async-start | bytes 4456448 | tf_op jit(solution)/shard_map/all_gather | solution.py:40
  12.2 290.8 %all-gather.11.cloned.1.call-start = ((), (), s32[]{:S(2)}) async-start(), calls=%async_computation.9 | async-start | bytes 4456448 | tf_op jit(solution)/shard_map/all_gather | solution.py:40
  12.8 392.1 %reduce-scatter.7.cloned.1.call-start = ((), (), s32[]{:S(2)}) async-start(), calls=%async_computation.5 | async-start | bytes 5242880 | tf_op jit(solution)/shard_map/reduce_scatter | solution.py:74
  15.2 293.4 %copy-start.5 = (bf16[1,256,1024]{1,2,0:T(8,128)(2,1)}, bf16[1,256,1024]{1,2,0:T(8,128)(2,1)S(1)}, u32[]{:S(2)}) copy-start(bf16[1,256,1024]{1,2,0:T(8,128)(2,1)S(1)} %copy.34) | copy-start | bytes 1572868
  15.5 234.0 %copy-start.6 = (bf16[1,256,1024]{1,2,0:T(8,128)(2,1)}, bf16[1,256,1024]{1,2,0:T(8,128)(2,1)S(1)}, u32[]{:S(2)}) copy-start(bf16[1,256,1024]{1,2,0:T(8,128)(2,1)S(1)} %copy.36) | copy-start | bytes 1572868
  88.6 155.3 %copy-start.34 = (f32[256]{0:T(256)}, f32[256]{0:T(256)S(1)}, u32[]{:S(2)}) copy-start(f32[256]{0:T(256)S(1)} %add_rsqrt_fusion) | copy-start | bytes 3076
  175.5 127.5 %copy-start.37 = (f32[256]{0:T(256)}, f32[256]{0:T(256)S(1)}, u32[]{:S(2)}) copy-start(f32[256]{0:T(256)S(1)} %add_rsqrt_fusion.1) | copy-start | bytes 3076
  243.8 4.8 copy-start.15
  249.4 59.8 %copy-start.26 = (f32[8,256]{1,0:T(8,128)}, f32[8,256]{1,0:T(8,128)S(1)}, u32[]{:S(2)}) copy-start(f32[8,256]{1,0:T(8,128)S(1)} %fusion.39) | copy-start | bytes 24580
  251.0 58.3 %copy-start.30 = (f32[8,256]{1,0:T(8,128)}, f32[8,256]{1,0:T(8,128)S(1)}, u32[]{:S(2)}) copy-start(f32[8,256]{1,0:T(8,128)S(1)} %neg.22) | copy-start | bytes 24580
  251.0 56.8 %copy-start.14 = (bf16[1,256,1024]{1,2,0:T(8,128)(2,1)S(1)}, bf16[1,256,1024]{1,2,0:T(8,128)(2,1)}, u32[]{:S(2)}) copy-start(bf16[1,256,1024]{1,2,0:T(8,128)(2,1)} %copy.56) | copy-start | bytes 1572868
  308.6 5.1 copy-start.28
  310.4 4.7 copy-start.16
  320.7 168.2 %reduce-scatter.5.cloned.1.call-start = ((), (), s32[]{:S(2)}) async-start(), calls=%async_computation.4 | async-start | bytes 5242880 | tf_op jit(solution)/shard_map/reduce_scatter | solution.py:74
  329.9 243.0 %reduce-scatter.9.cloned.1.call-start = ((), (), s32[]{:S(2)}) async-start(), calls=%async_computation.6 | async-start | bytes 4456448 | tf_op jit(solution)/shard_map/reduce_scatter | solution.py:86
  336.0 323.1 %reduce-scatter.11.cloned.1.call-start = ((), (), s32[]{:S(2)}) async-start(), calls=%async_computation.7 | async-start | bytes 4456448 | tf_op jit(solution)/shard_map/reduce_scatter | solution.py:86
  342.5 363.5 %all-reduce.4.cloned.1.call-start = ((), (), s32[]{:S(2)}) async-start(), calls=%async_computation.12 | async-start | bytes 1048576 | tf_op jit(solution)/shard_map/psum | solution.py:92
  342.8 6.7 copy-start
  342.8 6.7 copy-start.38
  357.0 5.6 copy-start.24
  407.1 252.0 %copy-start.12 = (bf16[256,2048]{1,0:T(8,128)(2,1)S(1)}, bf16[256,2048]{1,0:T(8,128)(2,1)}, u32[]{:S(2)}) copy-start(bf16[256,2048]{1,0:T(8,128)(2,1)} %reduce-scatter.7.cloned.1.call-done) | copy-start | bytes 3145732
  407.1 252.0 %copy-start.36 = (f32[256]{0:T(256)S(1)}, f32[256]{0:T(256)}, u32[]{:S(2)}) copy-start(f32[256]{0:T(256)} %copy-done.34) | copy-start | bytes 3076
  (28 other events, 78.0 us)
Sparse Core Ops, SparseCore 0:
  10.5 74.9 all-gather.12
  87.8 84.5 all-gather.8
  175.4 68.3 all-gather.14
  246.7 56.2 all-gather.10
  320.8 84.0 reduce-scatter.6
  407.5 81.3 reduce-scatter.4
  492.5 80.3 reduce-scatter.8
  577.0 82.0 reduce-scatter.10
  661.7 44.2 all-reduce.3
where the time goes:
time: 717 us; the launch traced here: 715 us
  waiting for transfers between devices  591 us (82%)
  matrix products  47.6 us (7%)
  other arithmetic  35.3 us (5%)
  local copies, waits for them, and re-layouts  17.1 us (2%)
  between operations  14.4 us (2%)
  blocking collectives  8.69 us (1%)
    reduce_scatter x2, waiting for transfers between devices, shards(): lax.psum_scatter(slab_term(jnp.int32(0), owned_count * lax.axis_size('lay...  159 us
    all_gather x2, waiting for transfers between devices, shards(): full_rows = lax.all_gather(hidden[depth], 'tensor', axis=1, tiled=True)  154 us
    all_gather x2, waiting for transfers between devices, fetch_slab(): return lax.all_gather(owned_rows, 'layer', axis=0, tiled=True)  120 us
    reduce_scatter x2, waiting for transfers between devices, shards(): lax.psum_scatter(spread_term.astype(jnp.bfloat16), 'tensor', scatter_dime...  115 us
    psum x1, waiting for transfers between devices, shards(): slab_grad = lax.psum(owned_grad, 'dp').astype(jnp.float32)  41.3 us
  transfers between devices with their start and end apart: 9, of which 9 were waited for; matrix products, arithmetic and copies ran while one was open for 11% of the time, Pallas kernels for 0%

commit v1 on v0

v1 whole, which is shorter than its diff:
```python
import functools

import jax
import jax.numpy as jnp
from jax import lax
from jax.experimental import pallas as pl
from jax.experimental.pallas import tpu as pltpu
from jax.sharding import PartitionSpec as P

D = 8192
HD = 128
GROUP = 8
SEQ = 256
EPSILON = 1e-05
BF16 = jnp.bfloat16
F32 = jnp.float32
AXES = ("layer", "dp", "tensor")
BLOCK = 256
VMEM_BYTES = 16 * 1024 * 1024
EXTRA = 16
LOG2E = 1.4426950408889634


def route(move):
    def flat(x, y, low, core, high):
        return ((x * 4 + y) * 4 + low * 2 + core) * 4 + high

    pairs = []
    for x in range(4):
        for y in range(4):
            for low in range(2):
                for core in range(2):
                    for high in range(4):
                        pairs.append((flat(x, y, low, core, high), flat(*move(x, y, low, core, high))))
    return pairs


def along_high(step):
    return route(lambda x, y, low, core, high: (x, y, low, core, (high + step) % 4))


CORE = route(lambda x, y, low, core, high: (x, y, low, 1 - core, high))
LOW = route(lambda x, y, low, core, high: (x, y, 1 - low, core, high))
BOTH = route(lambda x, y, low, core, high: (x, y, 1 - low, 1 - core, high))
SWAP = route(lambda x, y, low, core, high: (high, y, low, core, x))
STEPS = (1, 3, 2)


def shift(value, pairs):
    return lax.ppermute(value, AXES, pairs)


def after(value, *others):
    return lax.optimization_barrier((value, others))[0]


def dot(a, b, ca, cb):
    return lax.dot_general(a, b, (((ca,), (cb,)), ((), ())), preferred_element_type=F32)


def split_kernel(where, hidden, keep, send):
    core = where[2]
    for mine in range(2):

        @pl.when(core == mine)
        def _():
            for j in range(4):
                for out, half in ((keep, mine), (send, 1 - mine)):
                    first = (2 * j + half) * BLOCK
                    out[0, j] = hidden[0, :, first : first + BLOCK]


def norm_kernel(keep, sib, inverse, sib_inverse, normed, turned):
    for s, states, scale in ((0, keep, inverse), (1, sib, sib_inverse)):
        for j in range(4):
            part = (states[0, j].astype(F32) * scale[0]).astype(BF16)
            normed[0, s, j] = part
            turned[0, s, j] = part.T


def project_kernel(where, normed, blocks, out):
    out[0] = sum(dot(normed[0, 0, j], blocks[0, j], 1, 0) for j in range(4))


def merge_kernel(own, got, *outs):
    for k in range(4):
        outs[k][...] = own[k] + got[k]


def attend_kernel(has_old, *refs):
    parts, refs = refs[:4], refs[4:]
    query, cotangent = refs[:2]
    refs = refs[4:] if has_old else refs[2:]
    attended, query_grad, joined = refs
    projected = (parts[0][...] + parts[1][...]) + (parts[2][...] + parts[3][...])
    rounded = projected.astype(BF16)
    k, v = rounded[:, :HD], rounded[:, HD:]
    kt, vt = k.T, v.T
    to = lax.broadcasted_iota(jnp.int32, (SEQ, SEQ), 0)
    at = lax.broadcasted_iota(jnp.int32, (SEQ, SEQ), 1)
    key_grad = jnp.zeros((SEQ, HD), F32)
    value_grad = jnp.zeros((SEQ, HD), F32)
    for head in range(GROUP):
        columns = slice(head * HD, (head + 1) * HD)
        q, out_grad = query[0, :, columns], cotangent[0, :, columns]
        scores = jnp.where(at >= to, dot(k, q, 1, 1), -1e30)
        weights = jnp.exp2((scores - jnp.max(scores, axis=0, keepdims=True)) * (HD**-0.5 * LOG2E))
        weights = weights * (1.0 / jnp.sum(weights, axis=0, keepdims=True))
        held = weights.astype(BF16)
        attended[0, :, columns] = dot(vt, held, 1, 0).T.astype(BF16)
        weight_grad = dot(v, out_grad, 1, 1).astype(BF16).astype(F32)
        mean = jnp.sum(weights * weight_grad, axis=0, keepdims=True)
        score_grad = weights * (weight_grad - mean)
        upper = score_grad.astype(BF16)
        lower = (score_grad - upper.astype(F32)).astype(BF16)
        grad = dot(kt, upper, 1, 0) + dot(kt, lower, 1, 0)
        query_grad[0, :, columns] = (grad * HD**-0.5).T.astype(BF16)
        key_grad += dot(upper, q, 1, 0) + dot(lower, q, 1, 0)
        value_grad += dot(held, out_grad, 1, 0)
    grads = jnp.concatenate([key_grad * HD**-0.5, value_grad], axis=1).astype(BF16)
    joined[:SEQ] = grads
    shares = jnp.sum(grads.astype(F32) * projected, axis=1, keepdims=True)
    row = jnp.broadcast_to(shares, (SEQ, 128)).T[:EXTRA]
    at_row = lax.broadcasted_iota(jnp.int32, (EXTRA, SEQ), 0)
    terms = jnp.zeros((EXTRA, SEQ), F32)
    for index, term in enumerate(three(row)):
        terms = jnp.where(at_row == index, term.astype(F32), terms)
    joined[SEQ:] = terms.astype(BF16)


def three(value):
    terms = []
    for _ in range(3):
        terms.append(value.astype(BF16))
        value = value - terms[-1].astype(F32)
    return terms


def slab_kernel(where, turned, own, sib, out):
    k = lax.rem(pl.program_id(0) - where[3] + 4, 4)
    for j in range(4):
        term = dot(turned[0, 0, j], own[k, :SEQ], 1, 0).astype(BF16).astype(F32)
        term += dot(turned[0, 1, j], sib[k, :SEQ], 1, 0).astype(BF16).astype(F32)
        out[j] = term.astype(BF16)


def total_kernel(where, parts, moved, kept):
    total = parts[0].astype(F32)
    for k in range(1, 16):
        total += parts[k].astype(F32)

    @pl.when(pl.program_id(0) == 0)
    def _():
        moved[...] = total

    @pl.when(pl.program_id(0) == 1)
    def _():
        kept[...] = total


def spread_kernel(where, keep, sib, inverse, sib_inverse, own_heads, sib_heads, blocks, own_out, sib_out, products):
    @pl.when(pl.program_id(0) == 0)
    def _():
        for s, heads in enumerate((own_heads, sib_heads)):
            rows = [dot(heads[k, SEQ:], jnp.ones((EXTRA, BLOCK), BF16), 0, 0) for k in range(4)]
            products[s] = sum(rows) / D

    for s, heads, states, scale, out in (
        (1, sib_heads, sib, sib_inverse, sib_out),
        (0, own_heads, keep, inverse, own_out),
    ):
        spread = jnp.zeros((SEQ, BLOCK), F32)
        for b in range(4):
            term = dot(heads[lax.rem(b - where[3] + 4, 4), :SEQ], blocks[b, 0], 1, 1)
            spread += term.astype(BF16).astype(F32)
        scaled = states[0, 0].astype(F32) * scale[0]
        out[0] = (scale[0] * (spread - scaled * products[s])).astype(BF16)


def unsplit_kernel(has_old, where, keep, got, *refs):
    out = refs[-1]
    core = where[2]
    for mine in range(2):

        @pl.when(core == mine)
        def _():
            for j in range(4):
                for part, half in ((keep, mine), (got, 1 - mine)):
                    first = (2 * j + half) * BLOCK
                    out[0, :, first : first + BLOCK] = part[j]


def place_kernel(where, *refs):
    out = refs[8]
    core, low = where[2], where[4]
    for depth in range(2):
        for k in range(4):
            half = core if k % 2 == 0 else 1 - core
            quarter = low if k < 2 else 1 - low
            first = pl.multiple_of(half * 256 + quarter * 128, 128)
            out[depth, pl.ds(first, 128), :] = refs[4 * depth + k][...].astype(F32)


TILE = (SEQ, BLOCK)
ANY = pl.BlockSpec(memory_space=pl.ANY)


def shape(dims, dtype):
    return jax.ShapeDtypeStruct(dims, dtype)


def whole(*dims):
    return pl.BlockSpec(dims, lambda *_: (0,) * len(dims))


def layer_of(depth, *dims):
    return pl.BlockSpec((1,) + dims, lambda *_: (depth,) + (0,) * len(dims))


def run(kernel, grid, outs, in_specs, out_specs, args, scratch=(), aliases={}, megaflops=1, scalars=True):
    return pl.pallas_call(
        kernel,
        out_shape=outs,
        grid_spec=pltpu.PrefetchScalarGridSpec(
            num_scalar_prefetch=1 if scalars else 0,
            grid=(grid,),
            in_specs=in_specs,
            out_specs=out_specs,
            scratch_shapes=scratch,
        ),
        input_output_aliases=aliases,
        compiler_params=pltpu.CompilerParams(vmem_limit_bytes=VMEM_BYTES),
        cost_estimate=pl.CostEstimate(flops=megaflops * 10**6, bytes_accessed=6 << 20, transcendentals=0),
    )(*args)


def split(where, hidden):
    parts = pl.BlockSpec((1, 4) + TILE, lambda d, w: (d, 0, 0, 0))
    return run(
        split_kernel,
        2,
        [shape((2, 4) + TILE, BF16)] * 2,
        [pl.BlockSpec((1, SEQ, 2048), lambda d, w: (d, 0, 0))],
        [parts, parts],
        (where, hidden),
    )


def normalize(states):
    pair = pl.BlockSpec((1, 4) + TILE, lambda d: (d, 0, 0, 0))
    scale = pl.BlockSpec((1, SEQ, 1), lambda d: (d, 0, 0))
    out = pl.BlockSpec((1, 2, 4) + TILE, lambda d: (d, 0, 0, 0, 0))
    return run(
        norm_kernel,
        2,
        [shape((2, 2, 4) + TILE, BF16)] * 2,
        [pair, pair, scale, scale],
        [out, out],
        states,
        scalars=False,
    )


def project(depth, side, where, normed, blocks):
    return run(
        project_kernel,
        4,
        shape((4,) + TILE, F32),
        [
            pl.BlockSpec((1, 1, 4) + TILE, lambda k, w: (depth, side, 0, 0, 0)),
            pl.BlockSpec((1, 4) + TILE, lambda k, w: (lax.rem(k + w[3], 4), 0, 0, 0)),
        ],
        pl.BlockSpec((1,) + TILE, lambda k, w: (k, 0, 0)),
        (where, normed, blocks),
        megaflops=537,
    )


def merge(own, got):
    return run(
        merge_kernel,
        1,
        [shape(TILE, F32)] * 4,
        [whole(4, *TILE)] * 2,
        [whole(*TILE)] * 4,
        (own, got),
        scalars=False,
    )


def attend(depth, parts, queries, cotangent, old):
    heads = layer_of(depth, SEQ, GROUP * HD)
    return run(
        functools.partial(attend_kernel, bool(old)),
        1,
        [shape(queries.shape, BF16)] * 2 + [shape((SEQ + EXTRA, BLOCK), BF16)],
        [whole(*TILE)] * 4 + [heads] * 2 + [ANY] * len(old),
        [heads, heads, whole(SEQ + EXTRA, BLOCK)],
        (*parts, queries, cotangent, *old),
        aliases={6: 0, 7: 1} if old else {},
        megaflops=5000,
        scalars=False,
    )


def slab_terms(depth, where, turned, own, sib):
    return run(
        slab_kernel,
        4,
        shape((16,) + TILE, BF16),
        [layer_of(depth, 2, 4, *TILE)] + [whole(4, SEQ + EXTRA, BLOCK)] * 2,
        pl.BlockSpec((4,) + TILE, lambda b, w: (b, 0, 0)),
        (where, turned, own, sib),
        megaflops=1074,
    )


def plane_total(where, parts):
    quarter = pl.BlockSpec((16, 128, BLOCK), lambda s, w: (0, lax.rem(w[4] + 1 + s, 2), 0))
    return run(
        total_kernel,
        2,
        [shape((128, BLOCK), F32)] * 2,
        [quarter],
        [whole(128, BLOCK)] * 2,
        (where, parts),
    )


def spread_out(depth, where, states, own, sib, blocks):
    state = pl.BlockSpec((1, 1) + TILE, lambda j, w: (depth, j, 0, 0))
    row = pl.BlockSpec((4, 1) + TILE, lambda j, w: (0, j, 0, 0))
    out = pl.BlockSpec((1,) + TILE, lambda j, w: (j, 0, 0))
    return run(
        spread_kernel,
        4,
        [shape((4,) + TILE, BF16)] * 2,
        [state] * 2 + [layer_of(depth, SEQ, 1)] * 2 + [whole(4, SEQ + EXTRA, BLOCK)] * 2 + [row],
        [out, out],
        (where, *states, own, sib, blocks),
        [pltpu.VMEM((2,) + TILE, F32)],
        megaflops=1074,
    )


def unsplit(depth, where, keep, got, dims, old):
    return run(
        functools.partial(unsplit_kernel, bool(old)),
        1,
        shape(dims, BF16),
        [whole(4, *TILE)] * 2 + [ANY] * len(old),
        layer_of(depth, SEQ, 2048),
        (where, keep, got, *old),
        aliases={3: 0} if old else {},
    )


def place(where, quarters):
    return run(
        place_kernel,
        1,
        shape((2, 512, BLOCK), F32),
        [whole(128, BLOCK)] * 8,
        whole(2, 512, BLOCK),
        (where, *quarters),
    )


def shards(hidden, queries, cotangent, slabs):
    layer, dp, high = lax.axis_index("layer"), lax.axis_index("dp"), lax.axis_index("tensor")
    core, low = dp % 2, dp // 2
    where = jnp.stack([layer // 4, layer % 4, core, high, low]).astype(jnp.int32)

    half = lax.dynamic_slice_in_dim(slabs, core * BLOCK, BLOCK, 1)
    owned = shift(half[0], SWAP)
    keep, send = split(where, hidden)
    sib = shift(send, CORE)
    floats = hidden.astype(F32)
    squares = jnp.sum(floats * floats, axis=-1)
    owned = after(owned, send, squares)
    squares = squares + sum(shift(squares, along_high(k)) for k in (1, 2, 3))
    inverse = lax.rsqrt(squares / D + EPSILON)
    states = (keep, sib, inverse[..., None], shift(inverse, CORE)[..., None])
    normed, turned = normalize(states)

    blocks, sums = [], []
    for depth in range(2):
        sent = jnp.broadcast_to(owned, (16,) + TILE)
        if depth == 1:
            sent = after(sent, *sums[0])
        got = lax.all_to_all(sent, "layer", 0, 0, tiled=True)
        if depth == 0:
            owned = shift(after(half[1], sent), SWAP)
            got = after(got, owned)
        blocks.append(got.reshape((4, 4) + TILE))
        got = shift(project(depth, 1, where, normed, blocks[depth]), CORE)
        sums.append(merge(project(depth, 0, where, normed, blocks[depth]), got))

    old, hidden_grads, quarters = [], [], []
    for depth in range(2):
        arrived = {k: shift(sums[depth][k], along_high(k)) for k in STEPS}
        parts = [sums[depth][0]] + [arrived[k] for k in (1, 2, 3)]
        if depth == 1:
            parts = list(after(tuple(parts), own_out))
        attended, query_grads, joined = attend(depth, parts, queries, cotangent, old)
        old = [attended, query_grads]
        arrived = {k: shift(joined, along_high(-k)) for k in STEPS}
        own = jnp.stack([joined] + [arrived[k] for k in (1, 2, 3)])
        sib_heads = shift(own, CORE)
        if depth == 0:
            sums[1] = after(tuple(sums[1]), own)
        terms = slab_terms(depth, where, turned, own, sib_heads)
        own = after(own, terms)
        terms = lax.all_to_all(terms, "layer", 0, 0, tiled=True)
        own_out, sib_out = spread_out(depth, where, states, own, sib_heads, blocks[depth])
        got = shift(sib_out, CORE)
        hidden_grads = [unsplit(depth, where, own_out, got, hidden.shape, hidden_grads)]
        if depth == 1:
            terms = after(terms, own_out, *quarters)
        moved, kept = plane_total(where, terms)
        total = shift((kept + shift(moved, LOW)).astype(BF16), SWAP)
        quarters += [total] + [shift(total, pairs) for pairs in (CORE, LOW, BOTH)]
    return old[0], old[1], hidden_grads[0], place(where, quarters)


def solution(mesh):
    tokens = P(None, ("layer", "dp"), "tensor")
    rows = P(None, "layer", "tensor")
    return jax.shard_map(
        shards,
        mesh=mesh,
        in_specs=(tokens, tokens, tokens, rows),
        out_specs=(tokens, tokens, tokens, rows),
        check_vma=False,
    )
```

time: 717 us -> 271 us (0.38)
  waiting for transfers between devices: 591 us -> 72.2 us
  starting transfers between devices: 0.77 us -> 112 us
  Pallas kernels: 0 us -> 50 us
  matrix products: 47.6 us -> 0 us
  other arithmetic: 35.3 us -> 1.71 us
  local copies, waits for them, and re-layouts: 17.1 us -> 32.9 us
  between operations: 14.4 us -> 1.07 us
  blocking collectives: 8.69 us -> 0 us
    all_gather x4 -> x0, waiting for transfers between devices: 274 us -> none  [the longest x2 154 us: shards(): full_rows = lax.all_gather(hidden[depth], 'tensor', axis=1, tiled=True)]
    reduce_scatter x4 -> x0, waiting for transfers between devices: 274 us -> none  [the longest x2 159 us: shards(): lax.psum_scatter(slab_term(jnp.int32(0), owned_count * lax.axis_size('lay...]
    ppermute x0 -> x35, starting transfers between devices: none -> 81.6 us  [shift(): return lax.ppermute(value, AXES, pairs)]
    ppermute x0 -> x35, waiting for transfers between devices: none -> 71 us  [shift(): return lax.ppermute(value, AXES, pairs)]
    pallas_call x0 -> x19, Pallas kernels: none -> 50 us  [run(): pl.pallas_call(kernel, out_shape=outs, grid_spec=pltpu.PrefetchScalarGrid...]
    dot_general x18 -> x0, matrix products: 47.6 us -> none  [the longest x6 13.2 us: attend(): jnp.einsum('slhge,smhe->shglm', query_rows.astype(jnp.float32), key_rows....]
    psum x1 -> x0, waiting for transfers between devices: 41.3 us -> none  [shards(): slab_grad = lax.psum(owned_grad, 'dp').astype(jnp.float32)]
    all_to_all x0 -> x4, starting transfers between devices: none -> 30.7 us  [the longest x2 17.4 us: shards(): got = lax.all_to_all(sent, 'layer', 0, 0, tiled=True)]
  transfers between devices with their start and end apart: 9 -> 39, of which waited for: 9 -> 18; matrix products, arithmetic and copies ran while one was open for 11% -> 1% of each run, Pallas kernels for 0% -> 17%
where the time goes in v1:
time: 271 us; the launch traced here: 270 us
  starting transfers between devices  112 us (41%)
  waiting for transfers between devices  72.2 us (27%)
  Pallas kernels  50 us (18%)
  local copies, waits for them, and re-layouts  32.9 us (12%)
    ppermute x35, starting transfers between devices, shift(): return lax.ppermute(value, AXES, pairs)  81.6 us
    ppermute x35, waiting for transfers between devices, shift(): return lax.ppermute(value, AXES, pairs)  71 us
    pallas_call x19, Pallas kernels, run(): pl.pallas_call(kernel, out_shape=outs, grid_spec=pltpu.PrefetchScalarGrid...  50 us
    unnamed x84, local copies, waits for them, and re-layouts  27 us
    all_to_all x2, starting transfers between devices, shards(): got = lax.all_to_all(sent, 'layer', 0, 0, tiled=True)  17.4 us
    all_to_all x2, starting transfers between devices, shards(): terms = lax.all_to_all(terms, 'layer', 0, 0, tiled=True)  13.3 us
  transfers between devices with their start and end apart: 39, of which 18 were waited for; matrix products, arithmetic and copies ran while one was open for 1% of the time, Pallas kernels for 17%

profile of v1, /device:TPU:71, one launch (start us, length us, event | category | flops | bytes accessed | tf_op | source)
XLA Modules:
  0.0 270.3 jit_solution(17636541334112139472)
XLA Ops:
  2.3 7.8 %collective-permute-start.5 = (bf16[256,256]{1,0:T(8,128)(2,1)S(1)}, bf16[256,256]{1,0:T(8,128)(2,1)S(1)}, u32[]{:S(2)}, u32[]{:S(2)}) collective-permute-start(bf16[256,256]{1,0:T(8,128)(2,1)S(1)} %get-tuple-element.86), channel_id=1, source_target_pairs={{0,0},{1,64},{2,128},{3,192},{4,4},{5,68},{6,132},{7,196},{8,8},{9... | collective-permute-start | bytes 393224 | tf_op jit(solution)/shard_map/ppermute | solution.py:50
  16.4 9.2 %all-to-all-start = ((bf16[16,256,256]{2,1,0:T(8,128)(2,1)}), bf16[16,256,256]{2,1,0:T(8,128)(2,1)S(1)}, u32[]{:S(2)}, u32[]{:S(2)}) async-start(bf16[16,256,256]{2,1,0:T(8,128)(2,1)} %broadcast_in_dim.14), calls=%async_computation | async-start | bytes 4194304 | tf_op jit(solution)/shard_map/all_to_all | solution.py:391
  27.7 4.8 %collective-permute-start.2 = (f32[2,256]{1,0:T(2,128)S(1)}, f32[2,256]{1,0:T(2,128)S(1)}, u32[]{:S(2)}, u32[]{:S(2)}) collective-permute-start(f32[2,256]{1,0:T(2,128)S(1)} %multiply_reduce_fusion), channel_id=1, source_target_pairs={{0,2},{1,3},{2,0},{3,1},{4,6},{5,7},{6,4},{7,5},{8,10},{9,11},{10,... | collective-permute-start | bytes 6152 | tf_op jit(solution)/shard_map/ppermute | solution.py:50
  35.2 4.3 %collective-permute-start.6 = (bf16[256,256]{1,0:T(8,128)(2,1)}, bf16[256,256]{1,0:T(8,128)(2,1)S(1)}, u32[]{:S(2)}, u32[]{:S(2)}) collective-permute-start(bf16[256,256]{1,0:T(8,128)(2,1)} %get-tuple-element.49), channel_id=1, source_target_pairs={{0,0},{1,64},{2,128},{3,192},{4,4},{5,68},{6,132},{7,196},{8,8},{9... | collective-permute-start | bytes 393224 | tf_op jit(solution)/shard_map/ppermute | solution.py:50
  64.5 8.2 %all-to-all-start.1 = ((bf16[16,256,256]{2,1,0:T(8,128)(2,1)}), bf16[16,256,256]{2,1,0:T(8,128)(2,1)S(1)}, u32[]{:S(2)}, u32[]{:S(2)}) async-start(bf16[16,256,256]{2,1,0:T(8,128)(2,1)} %broadcast_in_dim.15), calls=%async_computation.1 | async-start | bytes 4194304 | tf_op jit(solution)/shard_map/all_to_all | solution.py:391
  72.7 4.8 %collective-permute-start.9 = (f32[256,256]{1,0:T(8,128)}, f32[256,256]{1,0:T(8,128)S(1)}, u32[]{:S(2)}, u32[]{:S(2)}) collective-permute-start(f32[256,256]{1,0:T(8,128)} %copy-done.41), channel_id=1, source_target_pairs={{0,1},{1,2},{2,3},{3,0},{4,5},{5,6},{6,7},{7,4},{8,9},{9,10},{10,1... | collective-permute-start | bytes 786440 | tf_op jit(solution)/shard_map/ppermute | solution.py:50
  81.7 6.5 %collective-permute-done.9.refs_1_ = f32[256,256]{1,0:T(8,128)S(1)} collective-permute-done((f32[256,256]{1,0:T(8,128)}, f32[256,256]{1,0:T(8,128)S(1)}, u32[]{:S(2)}, u32[]{:S(2)}) %collective-permute-start.9) | collective-permute-done | bytes 262176 | tf_op jit(solution)/shard_map/ppermute | solution.py:50
  88.1 14.1 %collective-permute-done.10.refs_2_ = f32[256,256]{1,0:T(8,128)S(1)} collective-permute-done((f32[256,256]{1,0:T(8,128)}, f32[256,256]{1,0:T(8,128)S(1)}, u32[]{:S(2)}, u32[]{:S(2)}) %collective-permute-start.10) | collective-permute-done | bytes 262176 | tf_op jit(solution)/shard_map/ppermute | solution.py:50
  106.5 5.6 %shard_map.83 = (bf16[2,256,1024]{2,1,0:T(8,128)(2,1)}, bf16[2,256,1024]{2,1,0:T(8,128)(2,1)}, bf16[272,256]{1,0:T(8,128)(2,1)S(1)}) custom-call(f32[256,256]{1,0:T(8,128)S(1)} %copy-done.38, f32[256,256]{1,0:T(8,128)S(1)} %collective-permute-done.9.refs_1_, f32[256,256]{1,0:T(8,128)S(1)} %collective-permute-done.10.refs_2_, ...), custom_call_target="tpu_custom_call" | custom-call | flops 5000000000 | bytes 6291456 | tf_op jit(solution)/shard_map/pallas_call | solution.py:221
  126.5 3.5 %collective-permute-done.12 = bf16[272,256]{1,0:T(8,128)(2,1)} collective-permute-done((bf16[272,256]{1,0:T(8,128)(2,1)S(1)}, bf16[272,256]{1,0:T(8,128)(2,1)}, u32[]{:S(2)}, u32[]{:S(2)}) %collective-permute-start.12) | collective-permute-done | bytes 139296 | tf_op jit(solution)/shard_map/ppermute | solution.py:50
  138.7 6.7 %all-to-all-start.2 = ((bf16[16,256,256]{2,1,0:T(8,128)(2,1)}), bf16[16,256,256]{2,1,0:T(8,128)(2,1)}, u32[]{:S(2)}, u32[]{:S(2)}) async-start(bf16[16,256,256]{2,1,0:T(8,128)(2,1)} %copy-done.11), calls=%async_computation.2 | async-start | bytes 4194304 | tf_op jit(solution)/shard_map/all_to_all | solution.py:414
  156.6 4.9 %shard_map.85 = (bf16[4,256,256]{2,1,0:T(8,128)(2,1)S(1)}, bf16[4,256,256]{2,1,0:T(8,128)(2,1)}) custom-call(s32[5]{0:T(128)S(1)} %stack.53.where, bf16[2,4,256,256]{3,2,1,0:T(8,128)(2,1)S(1)} %get-tuple-element.45.keep, bf16[2,4,256,256]{3,2,1,0:T(8,128)(2,1)} %collective-permute-done.sib, f32[2,256,1]{2,1,0:T(8,128)S(1)} %copy.17.inverse, ...), custom_call_target="tpu_custom_call" | custom-call | flops 1074000000 | bytes 6291456 | tf_op jit(solution)/shard_map/pallas_call | solution.py:221
  164.4 8.0 %collective-permute-done.16.refs_2_ = f32[256,256]{1,0:T(8,128)S(1)} collective-permute-done((f32[256,256]{1,0:T(8,128)S(1)}, f32[256,256]{1,0:T(8,128)S(1)}, u32[]{:S(2)}, u32[]{:S(2)}) %collective-permute-start.16) | collective-permute-done | bytes 262176 | tf_op jit(solution)/shard_map/ppermute | solution.py:50
  172.4 4.5 %collective-permute-done.17.refs_3_ = f32[256,256]{1,0:T(8,128)S(1)} collective-permute-done((f32[256,256]{1,0:T(8,128)S(1)}, f32[256,256]{1,0:T(8,128)S(1)}, u32[]{:S(2)}, u32[]{:S(2)}) %collective-permute-start.17) | collective-permute-done | bytes 262176 | tf_op jit(solution)/shard_map/ppermute | solution.py:50
  176.9 5.6 %shard_map.86 = (bf16[2,256,1024]{2,1,0:T(8,128)(2,1)}, bf16[2,256,1024]{2,1,0:T(8,128)(2,1)}, bf16[272,256]{1,0:T(8,128)(2,1)S(1)}) custom-call(f32[256,256]{1,0:T(8,128)S(1)} %get-tuple-element.68.refs_0_, f32[256,256]{1,0:T(8,128)S(1)} %collective-permute-done.15.refs_1_, ...), custom_call_target="tpu_custom_call", output_to_operand_aliasing={{0}: (6, {}), {1}: (7, {})} | custom-call | flops 5000000000 | bytes 6291456 | tf_op jit(solution)/shard_map/pallas_call | solution.py:221
  188.7 8.3 %collective-permute-done.20 = bf16[272,256]{1,0:T(8,128)(2,1)S(1)} collective-permute-done((bf16[272,256]{1,0:T(8,128)(2,1)S(1)}, bf16[272,256]{1,0:T(8,128)(2,1)S(1)}, u32[]{:S(2)}, u32[]{:S(2)}) %collective-permute-start.20) | collective-permute-done | bytes 139296 | tf_op jit(solution)/shard_map/ppermute | solution.py:50
  205.5 6.7 %all-to-all-start.3 = ((bf16[16,256,256]{2,1,0:T(8,128)(2,1)}), bf16[16,256,256]{2,1,0:T(8,128)(2,1)}, u32[]{:S(2)}, u32[]{:S(2)}) async-start(bf16[16,256,256]{2,1,0:T(8,128)(2,1)} %copy-done.12), calls=%async_computation.3 | async-start | bytes 4194304 | tf_op jit(solution)/shard_map/all_to_all | solution.py:414
  214.6 4.2 %collective-permute-done.25 = f32[128,256]{1,0:T(8,128)S(1)} collective-permute-done((f32[128,256]{1,0:T(8,128)S(1)}, f32[128,256]{1,0:T(8,128)S(1)}, u32[]{:S(2)}, u32[]{:S(2)}) %collective-permute-start.25) | collective-permute-done | bytes 131104 | tf_op jit(solution)/shard_map/ppermute | solution.py:50
  218.8 5.2 %collective-permute-start.26 = (bf16[128,256]{1,0:T(8,128)(2,1)S(1)}, bf16[128,256]{1,0:T(8,128)(2,1)S(1)}, u32[]{:S(2)}, u32[]{:S(2)}) collective-permute-start(bf16[128,256]{1,0:T(8,128)(2,1)S(1)} %add_convert_fusion.1), channel_id=1, source_target_pairs={{0,0},{1,64},{2,128},{3,192},{4,4},{5,68},{6,132},{7,196},{8,8},{9... | collective-permute-start | bytes 196616 | tf_op jit(solution)/shard_map/ppermute | solution.py:50
  226.1 4.4 %collective-permute-done.26.refs_0_ = bf16[128,256]{1,0:T(8,128)(2,1)S(1)} collective-permute-done((bf16[128,256]{1,0:T(8,128)(2,1)S(1)}, bf16[128,256]{1,0:T(8,128)(2,1)S(1)}, u32[]{:S(2)}, u32[]{:S(2)}) %collective-permute-start.26) | collective-permute-done | bytes 65568 | tf_op jit(solution)/shard_map/ppermute | solution.py:50
  234.5 4.9 %shard_map.88 = (bf16[4,256,256]{2,1,0:T(8,128)(2,1)S(1)}, bf16[4,256,256]{2,1,0:T(8,128)(2,1)}) custom-call(s32[5]{0:T(128)S(1)} %stack.53.where, bf16[2,4,256,256]{3,2,1,0:T(8,128)(2,1)S(1)} %get-tuple-element.45.keep, bf16[2,4,256,256]{3,2,1,0:T(8,128)(2,1)} %collective-permute-done.sib, f32[2,256,1]{2,1,0:T(8,128)S(1)} %copy.17.inverse, ...), custom_call_target="tpu_custom_call" | custom-call | flops 1074000000 | bytes 6291456 | tf_op jit(solution)/shard_map/pallas_call | solution.py:221
  244.4 4.5 %collective-permute-done.30 = f32[128,256]{1,0:T(8,128)S(1)} collective-permute-done((f32[128,256]{1,0:T(8,128)S(1)}, f32[128,256]{1,0:T(8,128)S(1)}, u32[]{:S(2)}, u32[]{:S(2)}) %collective-permute-start.30) | collective-permute-done | bytes 131104 | tf_op jit(solution)/shard_map/ppermute | solution.py:50
  249.0 6.1 %collective-permute-start.31 = (bf16[128,256]{1,0:T(8,128)(2,1)S(1)}, bf16[128,256]{1,0:T(8,128)(2,1)S(1)}, u32[]{:S(2)}, u32[]{:S(2)}) collective-permute-start(bf16[128,256]{1,0:T(8,128)(2,1)S(1)} %add_convert_fusion), channel_id=1, source_target_pairs={{0,0},{1,64},{2,128},{3,192},{4,4},{5,68},{6,132},{7,196},{8,8},{9... | collective-permute-start | bytes 196616 | tf_op jit(solution)/shard_map/ppermute | solution.py:50
  255.1 5.3 %collective-permute-done.31.refs_4_ = bf16[128,256]{1,0:T(8,128)(2,1)S(1)} collective-permute-done((bf16[128,256]{1,0:T(8,128)(2,1)S(1)}, bf16[128,256]{1,0:T(8,128)(2,1)S(1)}, u32[]{:S(2)}, u32[]{:S(2)}) %collective-permute-start.31) | collective-permute-done | bytes 65568 | tf_op jit(solution)/shard_map/ppermute | solution.py:50
  (169 shorter events, 120.9 us)
Async XLA Ops:
  2.3 12.6 %collective-permute-start.5 = (bf16[256,256]{1,0:T(8,128)(2,1)S(1)}, bf16[256,256]{1,0:T(8,128)(2,1)S(1)}, u32[]{:S(2)}, u32[]{:S(2)}) collective-permute-start(bf16[256,256]{1,0:T(8,128)(2,1)S(1)} %get-tuple-element.86), channel_id=1, source_target_pairs={{0,0},{1,64},{2,128},{3,192},{4,4},{5,68},{6,132},{7,196},{8,8},{9... | collective-permute-start | bytes 393224 | tf_op jit(solution)/shard_map/ppermute | solution.py:50
  16.4 33.8 %all-to-all-start = ((bf16[16,256,256]{2,1,0:T(8,128)(2,1)}), bf16[16,256,256]{2,1,0:T(8,128)(2,1)S(1)}, u32[]{:S(2)}, u32[]{:S(2)}) async-start(bf16[16,256,256]{2,1,0:T(8,128)(2,1)} %broadcast_in_dim.14), calls=%async_computation | async-start | bytes 4194304 | tf_op jit(solution)/shard_map/all_to_all | solution.py:391
  25.6 16.9 %collective-permute-start = (bf16[2,4,256,256]{3,2,1,0:T(8,128)(2,1)}, bf16[2,4,256,256]{3,2,1,0:T(8,128)(2,1)}, u32[]{:S(2)}, u32[]{:S(2)}) collective-permute-start(bf16[2,4,256,256]{3,2,1,0:T(8,128)(2,1)} %copy-done.36), channel_id=1, source_target_pairs={{0,4},{1,5},{2,6},{3,7},{4,0},{5,1},{6,2},{7,3},{8,12},{9,13},{10,... | collective-permute-start | bytes 3145736 | tf_op jit(solution)/shard_map/ppermute | solution.py:50
  27.7 11.8 %collective-permute-start.3 = (f32[2,256]{1,0:T(2,128)S(1)}, f32[2,256]{1,0:T(2,128)S(1)}, u32[]{:S(2)}, u32[]{:S(2)}) collective-permute-start(f32[2,256]{1,0:T(2,128)S(1)} %multiply_reduce_fusion), channel_id=1, source_target_pairs={{0,3},{1,0},{2,1},{3,2},{4,7},{5,4},{6,5},{7,6},{8,11},{9,8},{10,9... | collective-permute-start | bytes 6152 | tf_op jit(solution)/shard_map/ppermute | solution.py:50
  27.7 11.8 %collective-permute-start.2 = (f32[2,256]{1,0:T(2,128)S(1)}, f32[2,256]{1,0:T(2,128)S(1)}, u32[]{:S(2)}, u32[]{:S(2)}) collective-permute-start(f32[2,256]{1,0:T(2,128)S(1)} %multiply_reduce_fusion), channel_id=1, source_target_pairs={{0,2},{1,3},{2,0},{3,1},{4,6},{5,7},{6,4},{7,5},{8,10},{9,11},{10,... | collective-permute-start | bytes 6152 | tf_op jit(solution)/shard_map/ppermute | solution.py:50
  35.2 13.8 %collective-permute-start.6 = (bf16[256,256]{1,0:T(8,128)(2,1)}, bf16[256,256]{1,0:T(8,128)(2,1)S(1)}, u32[]{:S(2)}, u32[]{:S(2)}) collective-permute-start(bf16[256,256]{1,0:T(8,128)(2,1)} %get-tuple-element.49), channel_id=1, source_target_pairs={{0,0},{1,64},{2,128},{3,192},{4,4},{5,68},{6,132},{7,196},{8,8},{9... | collective-permute-start | bytes 393224 | tf_op jit(solution)/shard_map/ppermute | solution.py:50
  64.5 56.1 %all-to-all-start.1 = ((bf16[16,256,256]{2,1,0:T(8,128)(2,1)}), bf16[16,256,256]{2,1,0:T(8,128)(2,1)S(1)}, u32[]{:S(2)}, u32[]{:S(2)}) async-start(bf16[16,256,256]{2,1,0:T(8,128)(2,1)} %broadcast_in_dim.15), calls=%async_computation.1 | async-start | bytes 4194304 | tf_op jit(solution)/shard_map/all_to_all | solution.py:391
  72.7 15.4 %collective-permute-start.9 = (f32[256,256]{1,0:T(8,128)}, f32[256,256]{1,0:T(8,128)S(1)}, u32[]{:S(2)}, u32[]{:S(2)}) collective-permute-start(f32[256,256]{1,0:T(8,128)} %copy-done.41), channel_id=1, source_target_pairs={{0,1},{1,2},{2,3},{3,0},{4,5},{5,6},{6,7},{7,4},{8,9},{9,10},{10,1... | collective-permute-start | bytes 786440 | tf_op jit(solution)/shard_map/ppermute | solution.py:50
  77.5 24.7 %collective-permute-start.10 = (f32[256,256]{1,0:T(8,128)}, f32[256,256]{1,0:T(8,128)S(1)}, u32[]{:S(2)}, u32[]{:S(2)}) collective-permute-start(f32[256,256]{1,0:T(8,128)} %copy-done.40), channel_id=1, source_target_pairs={{0,2},{1,3},{2,0},{3,1},{4,6},{5,7},{6,4},{7,5},{8,10},{9,11},{10,... | collective-permute-start | bytes 786440 | tf_op jit(solution)/shard_map/ppermute | solution.py:50
  79.4 23.7 %collective-permute-start.11 = (f32[256,256]{1,0:T(8,128)}, f32[256,256]{1,0:T(8,128)S(1)}, u32[]{:S(2)}, u32[]{:S(2)}) collective-permute-start(f32[256,256]{1,0:T(8,128)} %copy-done.39), channel_id=1, source_target_pairs={{0,3},{1,0},{2,1},{3,2},{4,7},{5,4},{6,5},{7,6},{8,11},{9,8},{10,9... | collective-permute-start | bytes 786440 | tf_op jit(solution)/shard_map/ppermute | solution.py:50
  112.1 14.3 %collective-permute-start.14 = (bf16[272,256]{1,0:T(8,128)(2,1)S(1)}, bf16[272,256]{1,0:T(8,128)(2,1)}, u32[]{:S(2)}, u32[]{:S(2)}) collective-permute-start(bf16[272,256]{1,0:T(8,128)(2,1)S(1)} %get-tuple-element.60), channel_id=1, source_target_pairs={{0,1},{1,2},{2,3},{3,0},{4,5},{5,6},{6,7},{7,4},{8,9},{9,10},{10,1... | collective-permute-start | bytes 417800 | tf_op jit(solution)/shard_map/ppermute | solution.py:50
  114.7 11.7 %collective-permute-start.13 = (bf16[272,256]{1,0:T(8,128)(2,1)S(1)}, bf16[272,256]{1,0:T(8,128)(2,1)}, u32[]{:S(2)}, u32[]{:S(2)}) collective-permute-start(bf16[272,256]{1,0:T(8,128)(2,1)S(1)} %get-tuple-element.60), channel_id=1, source_target_pairs={{0,2},{1,3},{2,0},{3,1},{4,6},{5,7},{6,4},{7,5},{8,10},{9,11},{10,... | collective-permute-start | bytes 417800 | tf_op jit(solution)/shard_map/ppermute | solution.py:50
  118.2 11.8 %collective-permute-start.12 = (bf16[272,256]{1,0:T(8,128)(2,1)S(1)}, bf16[272,256]{1,0:T(8,128)(2,1)}, u32[]{:S(2)}, u32[]{:S(2)}) collective-permute-start(bf16[272,256]{1,0:T(8,128)(2,1)S(1)} %get-tuple-element.60), channel_id=1, source_target_pairs={{0,3},{1,0},{2,1},{3,2},{4,7},{5,4},{6,5},{7,6},{8,11},{9,8},{10,9... | collective-permute-start | bytes 417800 | tf_op jit(solution)/shard_map/ppermute | solution.py:50
  125.1 23.7 %collective-permute-start.8 = (f32[4,256,256]{2,1,0:T(8,128)}, f32[4,256,256]{2,1,0:T(8,128)}, u32[]{:S(2)}, u32[]{:S(2)}) collective-permute-start(f32[4,256,256]{2,1,0:T(8,128)} %shard_map.81), channel_id=1, source_target_pairs={{0,4},{1,5},{2,6},{3,7},{4,0},{5,1},{6,2},{7,3},{8,12},{9,13},{10,... | collective-permute-start | bytes 3145736 | tf_op jit(solution)/shard_map/ppermute | solution.py:50
  138.7 66.8 %all-to-all-start.2 = ((bf16[16,256,256]{2,1,0:T(8,128)(2,1)}), bf16[16,256,256]{2,1,0:T(8,128)(2,1)}, u32[]{:S(2)}, u32[]{:S(2)}) async-start(bf16[16,256,256]{2,1,0:T(8,128)(2,1)} %copy-done.11), calls=%async_computation.2 | async-start | bytes 4194304 | tf_op jit(solution)/shard_map/all_to_all | solution.py:414
  150.3 14.1 %collective-permute-start.15 = (f32[256,256]{1,0:T(8,128)S(1)}, f32[256,256]{1,0:T(8,128)S(1)}, u32[]{:S(2)}, u32[]{:S(2)}) collective-permute-start(f32[256,256]{1,0:T(8,128)S(1)} %get-tuple-element.62), channel_id=1, source_target_pairs={{0,1},{1,2},{2,3},{3,0},{4,5},{5,6},{6,7},{7,4},{8,9},{9,10},{10,1... | collective-permute-start | bytes 786440 | tf_op jit(solution)/shard_map/ppermute | solution.py:50
  152.7 19.7 %collective-permute-start.16 = (f32[256,256]{1,0:T(8,128)S(1)}, f32[256,256]{1,0:T(8,128)S(1)}, u32[]{:S(2)}, u32[]{:S(2)}) collective-permute-start(f32[256,256]{1,0:T(8,128)S(1)} %get-tuple-element.63), channel_id=1, source_target_pairs={{0,2},{1,3},{2,0},{3,1},{4,6},{5,7},{6,4},{7,5},{8,10},{9,11},{10,... | collective-permute-start | bytes 786440 | tf_op jit(solution)/shard_map/ppermute | solution.py:50
  156.0 20.9 %collective-permute-start.17 = (f32[256,256]{1,0:T(8,128)S(1)}, f32[256,256]{1,0:T(8,128)S(1)}, u32[]{:S(2)}, u32[]{:S(2)}) collective-permute-start(f32[256,256]{1,0:T(8,128)S(1)} %get-tuple-element.64), channel_id=1, source_target_pairs={{0,3},{1,0},{2,1},{3,2},{4,7},{5,4},{6,5},{7,6},{8,11},{9,8},{10,9... | collective-permute-start | bytes 786440 | tf_op jit(solution)/shard_map/ppermute | solution.py:50
  184.5 12.6 %collective-permute-start.20 = (bf16[272,256]{1,0:T(8,128)(2,1)S(1)}, bf16[272,256]{1,0:T(8,128)(2,1)S(1)}, u32[]{:S(2)}, u32[]{:S(2)}) collective-permute-start(bf16[272,256]{1,0:T(8,128)(2,1)S(1)} %get-tuple-element.76), channel_id=1, source_target_pairs={{0,2},{1,3},{2,0},{3,1},{4,6},{5,7},{6,4},{7,5},{8,10},{9,11},{10,... | collective-permute-start | bytes 417800 | tf_op jit(solution)/shard_map/ppermute | solution.py:50
  205.5 36.5 %all-to-all-start.3 = ((bf16[16,256,256]{2,1,0:T(8,128)(2,1)}), bf16[16,256,256]{2,1,0:T(8,128)(2,1)}, u32[]{:S(2)}, u32[]{:S(2)}) async-start(bf16[16,256,256]{2,1,0:T(8,128)(2,1)} %copy-done.12), calls=%async_computation.3 | async-start | bytes 4194304 | tf_op jit(solution)/shard_map/all_to_all | solution.py:414
  218.8 11.7 %collective-permute-start.26 = (bf16[128,256]{1,0:T(8,128)(2,1)S(1)}, bf16[128,256]{1,0:T(8,128)(2,1)S(1)}, u32[]{:S(2)}, u32[]{:S(2)}) collective-permute-start(bf16[128,256]{1,0:T(8,128)(2,1)S(1)} %add_convert_fusion.1), channel_id=1, source_target_pairs={{0,0},{1,64},{2,128},{3,192},{4,4},{5,68},{6,132},{7,196},{8,8},{9... | collective-permute-start | bytes 196616 | tf_op jit(solution)/shard_map/ppermute | solution.py:50
  224.0 40.3 %collective-permute-start.24 = (bf16[4,256,256]{2,1,0:T(8,128)(2,1)}, bf16[4,256,256]{2,1,0:T(8,128)(2,1)}, u32[]{:S(2)}, u32[]{:S(2)}) collective-permute-start(bf16[4,256,256]{2,1,0:T(8,128)(2,1)} %get-tuple-element.80), channel_id=1, source_target_pairs={{0,4},{1,5},{2,6},{3,7},{4,0},{5,1},{6,2},{7,3},{8,12},{9,13},{10,... | collective-permute-start | bytes 1572872 | tf_op jit(solution)/shard_map/ppermute | solution.py:50
  240.3 26.7 %collective-permute-start.23 = (bf16[4,256,256]{2,1,0:T(8,128)(2,1)}, bf16[4,256,256]{2,1,0:T(8,128)(2,1)S(1)}, u32[]{:S(2)}, u32[]{:S(2)}) collective-permute-start(bf16[4,256,256]{2,1,0:T(8,128)(2,1)} %get-tuple-element.79), channel_id=1, source_target_pairs={{0,4},{1,5},{2,6},{3,7},{4,0},{5,1},{6,2},{7,3},{8,12},{9,13},{10,... | collective-permute-start | bytes 1572872 | tf_op jit(solution)/shard_map/ppermute | solution.py:50
  249.0 11.4 %collective-permute-start.31 = (bf16[128,256]{1,0:T(8,128)(2,1)S(1)}, bf16[128,256]{1,0:T(8,128)(2,1)S(1)}, u32[]{:S(2)}, u32[]{:S(2)}) collective-permute-start(bf16[128,256]{1,0:T(8,128)(2,1)S(1)} %add_convert_fusion), channel_id=1, source_target_pairs={{0,0},{1,64},{2,128},{3,192},{4,4},{5,68},{6,132},{7,196},{8,8},{9... | collective-permute-start | bytes 196616 | tf_op jit(solution)/shard_map/ppermute | solution.py:50
  (57 other events, 365.2 us)

commit v2 on v1

--- a/solution.py
+++ b/solution.py
@@ -144,18 +144,11 @@
         out[j] = term.astype(BF16)
 
 
-def total_kernel(where, parts, moved, kept):
+def total_kernel(parts, out):
     total = parts[0].astype(F32)
     for k in range(1, 16):
         total += parts[k].astype(F32)
-
-    @pl.when(pl.program_id(0) == 0)
-    def _():
-        moved[...] = total
-
-    @pl.when(pl.program_id(0) == 1)
-    def _():
-        kept[...] = total
+    out[...] = total.astype(BF16)
 
 
 def spread_kernel(where, keep, sib, inverse, sib_inverse, own_heads, sib_heads, blocks, own_out, sib_out, products):
@@ -192,13 +185,11 @@
 
 def place_kernel(where, *refs):
     out = refs[8]
-    core, low = where[2], where[4]
     for depth in range(2):
-        for k in range(4):
-            half = core if k % 2 == 0 else 1 - core
-            quarter = low if k < 2 else 1 - low
-            first = pl.multiple_of(half * 256 + quarter * 128, 128)
-            out[depth, pl.ds(first, 128), :] = refs[4 * depth + k][...].astype(F32)
+        for k in range(2):
+            first = pl.multiple_of((where[2] if k == 0 else 1 - where[2]) * BLOCK, BLOCK)
+            near, far = refs[4 * depth + k], refs[4 * depth + 2 + k]
+            out[depth, pl.ds(first, BLOCK), :] = near[...].astype(F32) + far[...].astype(F32)
 
 
 TILE = (SEQ, BLOCK)
@@ -315,15 +306,15 @@
     )
 
 
-def plane_total(where, parts):
-    quarter = pl.BlockSpec((16, 128, BLOCK), lambda s, w: (0, lax.rem(w[4] + 1 + s, 2), 0))
+def plane_total(parts):
     return run(
         total_kernel,
-        2,
-        [shape((128, BLOCK), F32)] * 2,
-        [quarter],
-        [whole(128, BLOCK)] * 2,
-        (where, parts),
+        4,
+        shape(TILE, BF16),
+        [pl.BlockSpec((16, 64, BLOCK), lambda s: (0, s, 0))],
+        pl.BlockSpec((64, BLOCK), lambda s: (s, 0)),
+        (parts,),
+        scalars=False,
     )
 
 
@@ -360,7 +351,7 @@
         place_kernel,
         1,
         shape((2, 512, BLOCK), F32),
-        [whole(128, BLOCK)] * 8,
+        [whole(*TILE)] * 8,
         whole(2, 512, BLOCK),
         (where, *quarters),
     )
@@ -383,44 +374,61 @@
     states = (keep, sib, inverse[..., None], shift(inverse, CORE)[..., None])
     normed, turned = normalize(states)
 
-    blocks, sums = [], []
-    for depth in range(2):
-        sent = jnp.broadcast_to(owned, (16,) + TILE)
-        if depth == 1:
-            sent = after(sent, *sums[0])
-        got = lax.all_to_all(sent, "layer", 0, 0, tiled=True)
-        if depth == 0:
-            owned = shift(after(half[1], sent), SWAP)
-            got = after(got, owned)
-        blocks.append(got.reshape((4, 4) + TILE))
-        got = shift(project(depth, 1, where, normed, blocks[depth]), CORE)
-        sums.append(merge(project(depth, 0, where, normed, blocks[depth]), got))
-
-    old, hidden_grads, quarters = [], [], []
-    for depth in range(2):
-        arrived = {k: shift(sums[depth][k], along_high(k)) for k in STEPS}
-        parts = [sums[depth][0]] + [arrived[k] for k in (1, 2, 3)]
-        if depth == 1:
-            parts = list(after(tuple(parts), own_out))
-        attended, query_grads, joined = attend(depth, parts, queries, cotangent, old)
-        old = [attended, query_grads]
+    def fetch(sent):
+        return lax.all_to_all(sent, "layer", 0, 0, tiled=True)
+
+    def partial(depth, part):
+        away = shift(project(depth, 1, where, normed, part), CORE)
+        return merge(project(depth, 0, where, normed, part), away)
+
+    def reduce_heads(sums):
+        arrived = {k: shift(sums[k], along_high(k)) for k in STEPS}
+        return [sums[0]] + [arrived[k] for k in (1, 2, 3)]
+
+    def gather_heads(joined):
         arrived = {k: shift(joined, along_high(-k)) for k in STEPS}
-        own = jnp.stack([joined] + [arrived[k] for k in (1, 2, 3)])
-        sib_heads = shift(own, CORE)
-        if depth == 0:
-            sums[1] = after(tuple(sums[1]), own)
-        terms = slab_terms(depth, where, turned, own, sib_heads)
-        own = after(own, terms)
-        terms = lax.all_to_all(terms, "layer", 0, 0, tiled=True)
-        own_out, sib_out = spread_out(depth, where, states, own, sib_heads, blocks[depth])
-        got = shift(sib_out, CORE)
-        hidden_grads = [unsplit(depth, where, own_out, got, hidden.shape, hidden_grads)]
-        if depth == 1:
-            terms = after(terms, own_out, *quarters)
-        moved, kept = plane_total(where, terms)
-        total = shift((kept + shift(moved, LOW)).astype(BF16), SWAP)
-        quarters += [total] + [shift(total, pairs) for pairs in (CORE, LOW, BOTH)]
-    return old[0], old[1], hidden_grads[0], place(where, quarters)
+        return jnp.stack([joined] + [arrived[k] for k in (1, 2, 3)])
+
+    def spread(placed):
+        return [placed] + [shift(placed, pairs) for pairs in (CORE, LOW, BOTH)]
+
+    sent = jnp.broadcast_to(owned, (16,) + TILE)
+    blocks = fetch(sent)
+    owned = shift(after(half[1], sent), SWAP)
+    sent = jnp.broadcast_to(owned, (16,) + TILE)
+    blocks0 = after(blocks, owned).reshape((4, 4) + TILE)
+    sums = partial(0, blocks0)
+    sent = after(sent, *sums)
+    parts = reduce_heads(sums)
+    parts, blocks1 = lax.optimization_barrier((parts, fetch(sent)))
+    blocks1 = blocks1.reshape((4, 4) + TILE)
+    attended, query_grads, joined = attend(0, parts, queries, cotangent, [])
+    sums = partial(1, blocks1)
+
+    joined, parts = lax.optimization_barrier((joined, reduce_heads(sums)))
+    own0 = gather_heads(joined)
+    attended, query_grads, joined = attend(1, parts, queries, cotangent, [attended, query_grads])
+    own0, joined = lax.optimization_barrier((own0, joined))
+    sib0 = shift(own0, CORE)
+    terms0 = slab_terms(0, where, turned, own0, sib0)
+    own0, sib0 = after((own0, sib0), terms0)
+    terms0 = fetch(terms0)
+
+    own1 = gather_heads(joined)
+    sib1 = shift(own1, CORE)
+    terms1 = slab_terms(1, where, turned, own1, sib1)
+    own1, sib1, own0 = after((own1, sib1, own0), terms1)
+    terms1 = fetch(terms1)
+    own_out, sib_out = spread_out(0, where, states, own0, sib0, blocks0)
+    hidden_grads = unsplit(0, where, own_out, shift(sib_out, CORE), hidden.shape, [])
+    own_out, sib_out = spread_out(1, where, states, own1, sib1, blocks1)
+    hidden_grads = unsplit(1, where, own_out, shift(sib_out, CORE), hidden.shape, [hidden_grads])
+
+    total = after(plane_total(terms0), own_out)
+    quarters = spread(shift(total, SWAP))
+    total = plane_total(after(terms1, total, hidden_grads))
+    quarters += spread(shift(total, SWAP))
+    return attended, query_grads, hidden_grads, place(where, quarters)
 
 
 def solution(mesh):

time: 271 us -> 267 us (0.985); the launches traced: 270 us -> 262 us
  waiting for transfers between devices: 72.2 us -> 63.3 us
  starting transfers between devices: 112 us -> 116 us
    ppermute x35 -> x33, waiting for transfers between devices: 71 us -> 61 us  [shift(): return lax.ppermute(value, AXES, pairs)]
    ppermute x35 -> x33, starting transfers between devices: 81.6 us -> 84.1 us  [shift(): return lax.ppermute(value, AXES, pairs)]
    unnamed x84 -> x68, local copies, waits for them, and re-layouts: 27 us -> 25.2 us
  transfers between devices with their start and end apart: 39 -> 37, of which waited for: 18 -> 19; matrix products, arithmetic and copies ran while one was open for 1% -> 1% of each run, Pallas kernels for 17% -> 15%
where the time goes in v2:
time: 267 us; the launch traced here: 262 us
  starting transfers between devices  116 us (43%)
  waiting for transfers between devices  63.3 us (24%)
  Pallas kernels  49.8 us (19%)
  local copies, waits for them, and re-layouts  31 us (12%)
    ppermute x33, starting transfers between devices, shift(): return lax.ppermute(value, AXES, pairs)  84.1 us
    ppermute x33, waiting for transfers between devices, shift(): return lax.ppermute(value, AXES, pairs)  61 us
    pallas_call x19, Pallas kernels, run(): pl.pallas_call(kernel, out_shape=outs, grid_spec=pltpu.PrefetchScalarGrid...  49.8 us
    all_to_all x4, starting transfers between devices, fetch(): return lax.all_to_all(sent, 'layer', 0, 0, tiled=True)  32.4 us
    unnamed x68, local copies, waits for them, and re-layouts  25.2 us
  transfers between devices with their start and end apart: 37, of which 19 were waited for; matrix products, arithmetic and copies ran while one was open for 1% of the time, Pallas kernels for 15%

profile of v2, /device:TPU:71, one launch (start us, length us, event | category | flops | bytes accessed | tf_op | source)
XLA Modules:
  0.0 262.2 jit_solution(10962705138704863844)
XLA Ops:
  2.3 7.8 %collective-permute-start.5 = (bf16[256,256]{1,0:T(8,128)(2,1)S(1)}, bf16[256,256]{1,0:T(8,128)(2,1)S(1)}, u32[]{:S(2)}, u32[]{:S(2)}) collective-permute-start(bf16[256,256]{1,0:T(8,128)(2,1)S(1)} %get-tuple-element.95), channel_id=1, source_target_pairs={{0,0},{1,64},{2,128},{3,192},{4,4},{5,68},{6,132},{7,196},{8,8},{9... | collective-permute-start | bytes 393224 | tf_op jit(solution)/shard_map/ppermute | solution.py:50
  16.4 9.2 %all-to-all-start = ((bf16[16,256,256]{2,1,0:T(8,128)(2,1)}), bf16[16,256,256]{2,1,0:T(8,128)(2,1)S(1)}, u32[]{:S(2)}, u32[]{:S(2)}) async-start(bf16[16,256,256]{2,1,0:T(8,128)(2,1)} %broadcast_in_dim.14), calls=%async_computation | async-start | bytes 4194304 | tf_op jit(solution)/shard_map/all_to_all | solution.py:378
  27.7 4.8 %collective-permute-start.2 = (f32[2,256]{1,0:T(2,128)S(1)}, f32[2,256]{1,0:T(2,128)S(1)}, u32[]{:S(2)}, u32[]{:S(2)}) collective-permute-start(f32[2,256]{1,0:T(2,128)S(1)} %multiply_reduce_fusion), channel_id=1, source_target_pairs={{0,2},{1,3},{2,0},{3,1},{4,6},{5,7},{6,4},{7,5},{8,10},{9,11},{10,... | collective-permute-start | bytes 6152 | tf_op jit(solution)/shard_map/ppermute | solution.py:50
  35.1 4.3 %collective-permute-start.6 = (bf16[256,256]{1,0:T(8,128)(2,1)}, bf16[256,256]{1,0:T(8,128)(2,1)S(1)}, u32[]{:S(2)}, u32[]{:S(2)}) collective-permute-start(bf16[256,256]{1,0:T(8,128)(2,1)} %get-tuple-element.53), channel_id=1, source_target_pairs={{0,0},{1,64},{2,128},{3,192},{4,4},{5,68},{6,132},{7,196},{8,8},{9... | collective-permute-start | bytes 393224 | tf_op jit(solution)/shard_map/ppermute | solution.py:50
  53.5 3.4 %collective-permute-start.7 = (f32[4,256,256]{2,1,0:T(8,128)S(1)}, f32[4,256,256]{2,1,0:T(8,128)S(1)}, u32[]{:S(2)}, u32[]{:S(2)}) collective-permute-start(f32[4,256,256]{2,1,0:T(8,128)S(1)} %shard_map.78), channel_id=1, source_target_pairs={{0,4},{1,5},{2,6},{3,7},{4,0},{5,1},{6,2},{7,3},{8,12},{9,13},{10,... | collective-permute-start | bytes 3145736 | tf_op jit(solution)/shard_map/ppermute | solution.py:50
  63.7 8.6 %all-to-all-start.1 = ((bf16[16,256,256]{2,1,0:T(8,128)(2,1)}), bf16[16,256,256]{2,1,0:T(8,128)(2,1)}, u32[]{:S(2)}, u32[]{:S(2)}) async-start(bf16[16,256,256]{2,1,0:T(8,128)(2,1)} %broadcast_in_dim.15), calls=%async_computation.1 | async-start | bytes 4194304 | tf_op jit(solution)/shard_map/all_to_all | solution.py:378
  72.3 4.4 %collective-permute-start.8 = (f32[256,256]{1,0:T(8,128)}, f32[256,256]{1,0:T(8,128)S(1)}, u32[]{:S(2)}, u32[]{:S(2)}) collective-permute-start(f32[256,256]{1,0:T(8,128)} %copy-done.33), channel_id=1, source_target_pairs={{0,1},{1,2},{2,3},{3,0},{4,5},{5,6},{6,7},{7,4},{8,9},{9,10},{10,1... | collective-permute-start | bytes 786440 | tf_op jit(solution)/shard_map/ppermute | solution.py:50
  80.9 5.1 %collective-permute-done.8.refs_1_ = f32[256,256]{1,0:T(8,128)S(1)} collective-permute-done((f32[256,256]{1,0:T(8,128)}, f32[256,256]{1,0:T(8,128)S(1)}, u32[]{:S(2)}, u32[]{:S(2)}) %collective-permute-start.8) | collective-permute-done | bytes 262176 | tf_op jit(solution)/shard_map/ppermute | solution.py:50
  86.7 14.8 %collective-permute-done.9.refs_2_ = f32[256,256]{1,0:T(8,128)S(1)} collective-permute-done((f32[256,256]{1,0:T(8,128)}, f32[256,256]{1,0:T(8,128)S(1)}, u32[]{:S(2)}, u32[]{:S(2)}) %collective-permute-start.9) | collective-permute-done | bytes 262176 | tf_op jit(solution)/shard_map/ppermute | solution.py:50
  104.7 3.6 %shard_map.82 = f32[4,256,256]{2,1,0:T(8,128)S(1)} custom-call(s32[5]{0:T(128)S(1)} %stack.53.where, bf16[2,2,4,256,256]{4,3,2,1,0:T(8,128)(2,1)S(1)} %copy-done.2, bf16[4,4,256,256]{3,2,1,0:T(8,128)(2,1)} %bitcast.10.blocks), custom_call_target="tpu_custom_call" | custom-call | flops 537000000 | bytes 6291456 | tf_op jit(solution)/shard_map/pallas_call | solution.py:212
  109.9 3.6 %shard_map.81.own = f32[4,256,256]{2,1,0:T(8,128)S(1)} custom-call(s32[5]{0:T(128)S(1)} %stack.53.where, bf16[2,2,4,256,256]{4,3,2,1,0:T(8,128)(2,1)S(1)} %copy-done.2, bf16[4,4,256,256]{3,2,1,0:T(8,128)(2,1)} %bitcast.10.blocks), custom_call_target="tpu_custom_call" | custom-call | flops 537000000 | bytes 6291456 | tf_op jit(solution)/shard_map/pallas_call | solution.py:212
  121.3 5.6 %shard_map.80 = (bf16[2,256,1024]{2,1,0:T(8,128)(2,1)}, bf16[2,256,1024]{2,1,0:T(8,128)(2,1)}, bf16[272,256]{1,0:T(8,128)(2,1)S(1)}) custom-call(f32[256,256]{1,0:T(8,128)S(1)} %copy-done.24, f32[256,256]{1,0:T(8,128)S(1)} %copy-done.26, f32[256,256]{1,0:T(8,128)S(1)} %copy-done.28, f32[256,256]{1,0:T(8,128)S(1)} %copy-done.30, ...), custom_call_target="tpu_custom_call" | custom-call | flops 5000000000 | bytes 6291456 | tf_op jit(solution)/shard_map/pallas_call | solution.py:212
  127.0 15.6 %collective-permute-done.13.refs_2_ = f32[256,256]{1,0:T(8,128)S(1)} collective-permute-done((f32[256,256]{1,0:T(8,128)S(1)}, f32[256,256]{1,0:T(8,128)S(1)}, u32[]{:S(2)}, u32[]{:S(2)}) %collective-permute-start.13) | collective-permute-done | bytes 262176 | tf_op jit(solution)/shard_map/ppermute | solution.py:50
  150.5 5.6 %shard_map.84 = (bf16[2,256,1024]{2,1,0:T(8,128)(2,1)}, bf16[2,256,1024]{2,1,0:T(8,128)(2,1)}, bf16[272,256]{1,0:T(8,128)(2,1)S(1)}) custom-call(f32[256,256]{1,0:T(8,128)S(1)} %get-tuple-element.70.refs_0_, f32[256,256]{1,0:T(8,128)S(1)} %collective-permute-done.12.refs_1_, ...), custom_call_target="tpu_custom_call", output_to_operand_aliasing={{0}: (6, {}), {1}: (7, {})} | custom-call | flops 5000000000 | bytes 6291456 | tf_op jit(solution)/shard_map/pallas_call | solution.py:212
  165.7 7.9 %all-to-all-start.2 = ((bf16[16,256,256]{2,1,0:T(8,128)(2,1)}), bf16[16,256,256]{2,1,0:T(8,128)(2,1)}, u32[]{:S(2)}, u32[]{:S(2)}) async-start(bf16[16,256,256]{2,1,0:T(8,128)(2,1)} %copy-done.9), calls=%async_computation.2 | async-start | bytes 4194304 | tf_op jit(solution)/shard_map/all_to_all | solution.py:378
  180.8 6.6 %collective-permute-done.19 = bf16[272,256]{1,0:T(8,128)(2,1)S(1)} collective-permute-done((bf16[272,256]{1,0:T(8,128)(2,1)S(1)}, bf16[272,256]{1,0:T(8,128)(2,1)S(1)}, u32[]{:S(2)}, u32[]{:S(2)}) %collective-permute-start.19) | collective-permute-done | bytes 139296 | tf_op jit(solution)/shard_map/ppermute | solution.py:50
  187.4 4.1 %collective-permute-done.18 = bf16[272,256]{1,0:T(8,128)(2,1)S(1)} collective-permute-done((bf16[272,256]{1,0:T(8,128)(2,1)S(1)}, bf16[272,256]{1,0:T(8,128)(2,1)S(1)}, u32[]{:S(2)}, u32[]{:S(2)}) %collective-permute-start.18) | collective-permute-done | bytes 139296 | tf_op jit(solution)/shard_map/ppermute | solution.py:50
  201.6 6.8 %all-to-all-start.3 = ((bf16[16,256,256]{2,1,0:T(8,128)(2,1)}), bf16[16,256,256]{2,1,0:T(8,128)(2,1)}, u32[]{:S(2)}, u32[]{:S(2)}) async-start(bf16[16,256,256]{2,1,0:T(8,128)(2,1)} %copy-done.8), calls=%async_computation.3 | async-start | bytes 4194304 | tf_op jit(solution)/shard_map/all_to_all | solution.py:378
  211.4 4.4 %shard_map.88 = (bf16[4,256,256]{2,1,0:T(8,128)(2,1)S(1)}, bf16[4,256,256]{2,1,0:T(8,128)(2,1)S(1)}) custom-call(s32[5]{0:T(128)S(1)} %stack.53.where, bf16[2,4,256,256]{3,2,1,0:T(8,128)(2,1)S(1)} %get-tuple-element.49.keep, bf16[2,4,256,256]{3,2,1,0:T(8,128)(2,1)} %collective-permute-done.sib, f32[2,256,1]{2,1,0:T(8,128)S(1)} %copy.17.inverse, ...), custom_call_target="tpu_custom_call" | custom-call | flops 1074000000 | bytes 6291456 | tf_op jit(solution)/shard_map/pallas_call | solution.py:212
  217.7 4.8 %shard_map.87 = (bf16[4,256,256]{2,1,0:T(8,128)(2,1)S(1)}, bf16[4,256,256]{2,1,0:T(8,128)(2,1)S(1)}) custom-call(s32[5]{0:T(128)S(1)} %stack.53.where, bf16[2,4,256,256]{3,2,1,0:T(8,128)(2,1)S(1)} %get-tuple-element.49.keep, bf16[2,4,256,256]{3,2,1,0:T(8,128)(2,1)} %collective-permute-done.sib, f32[2,256,1]{2,1,0:T(8,128)S(1)} %copy.17.inverse, ...), custom_call_target="tpu_custom_call" | custom-call | flops 1074000000 | bytes 6291456 | tf_op jit(solution)/shard_map/pallas_call | solution.py:212
  225.2 6.9 %collective-permute-start.25 = (bf16[256,256]{1,0:T(8,128)(2,1)S(1)}, bf16[256,256]{1,0:T(8,128)(2,1)S(1)}, u32[]{:S(2)}, u32[]{:S(2)}) collective-permute-start(bf16[256,256]{1,0:T(8,128)(2,1)S(1)} %shard_map.91), channel_id=1, source_target_pairs={{0,0},{1,64},{2,128},{3,192},{4,4},{5,68},{6,132},{7,196},{8,8},{9... | collective-permute-start | bytes 393224 | tf_op jit(solution)/shard_map/ppermute | solution.py:50
  237.9 4.7 %collective-permute-start.29 = (bf16[256,256]{1,0:T(8,128)(2,1)S(1)}, bf16[256,256]{1,0:T(8,128)(2,1)S(1)}, u32[]{:S(2)}, u32[]{:S(2)}) collective-permute-start(bf16[256,256]{1,0:T(8,128)(2,1)S(1)} %shard_map.92), channel_id=1, source_target_pairs={{0,0},{1,64},{2,128},{3,192},{4,4},{5,68},{6,132},{7,196},{8,8},{9... | collective-permute-start | bytes 393224 | tf_op jit(solution)/shard_map/ppermute | solution.py:50
  242.6 4.3 %collective-permute-start.28 = (bf16[256,256]{1,0:T(8,128)(2,1)S(1)}, bf16[256,256]{1,0:T(8,128)(2,1)S(1)}, u32[]{:S(2)}, u32[]{:S(2)}) collective-permute-start(bf16[256,256]{1,0:T(8,128)(2,1)S(1)} %collective-permute-done.25.refs_0_), channel_id=1, source_target_pairs={{0,12},{1,13},{2,14},{3,15},{4,8},{5,9},{6,10},{7,11},{8,4},{9,5},... | collective-permute-start | bytes 393224 | tf_op jit(solution)/shard_map/ppermute | solution.py:50
  256.4 4.2 %collective-permute-done.31.refs_6_ = bf16[256,256]{1,0:T(8,128)(2,1)S(1)} collective-permute-done((bf16[256,256]{1,0:T(8,128)(2,1)S(1)}, bf16[256,256]{1,0:T(8,128)(2,1)S(1)}, u32[]{:S(2)}, u32[]{:S(2)}) %collective-permute-start.31) | collective-permute-done | bytes 131104 | tf_op jit(solution)/shard_map/ppermute | solution.py:50
  (147 shorter events, 110.0 us)
Async XLA Ops:
  2.3 12.6 %collective-permute-start.5 = (bf16[256,256]{1,0:T(8,128)(2,1)S(1)}, bf16[256,256]{1,0:T(8,128)(2,1)S(1)}, u32[]{:S(2)}, u32[]{:S(2)}) collective-permute-start(bf16[256,256]{1,0:T(8,128)(2,1)S(1)} %get-tuple-element.95), channel_id=1, source_target_pairs={{0,0},{1,64},{2,128},{3,192},{4,4},{5,68},{6,132},{7,196},{8,8},{9... | collective-permute-start | bytes 393224 | tf_op jit(solution)/shard_map/ppermute | solution.py:50
  16.4 33.8 %all-to-all-start = ((bf16[16,256,256]{2,1,0:T(8,128)(2,1)}), bf16[16,256,256]{2,1,0:T(8,128)(2,1)S(1)}, u32[]{:S(2)}, u32[]{:S(2)}) async-start(bf16[16,256,256]{2,1,0:T(8,128)(2,1)} %broadcast_in_dim.14), calls=%async_computation | async-start | bytes 4194304 | tf_op jit(solution)/shard_map/all_to_all | solution.py:378
  25.6 16.9 %collective-permute-start = (bf16[2,4,256,256]{3,2,1,0:T(8,128)(2,1)}, bf16[2,4,256,256]{3,2,1,0:T(8,128)(2,1)}, u32[]{:S(2)}, u32[]{:S(2)}) collective-permute-start(bf16[2,4,256,256]{3,2,1,0:T(8,128)(2,1)} %copy-done.22), channel_id=1, source_target_pairs={{0,4},{1,5},{2,6},{3,7},{4,0},{5,1},{6,2},{7,3},{8,12},{9,13},{10,... | collective-permute-start | bytes 3145736 | tf_op jit(solution)/shard_map/ppermute | solution.py:50
  27.7 11.8 %collective-permute-start.3 = (f32[2,256]{1,0:T(2,128)S(1)}, f32[2,256]{1,0:T(2,128)S(1)}, u32[]{:S(2)}, u32[]{:S(2)}) collective-permute-start(f32[2,256]{1,0:T(2,128)S(1)} %multiply_reduce_fusion), channel_id=1, source_target_pairs={{0,3},{1,0},{2,1},{3,2},{4,7},{5,4},{6,5},{7,6},{8,11},{9,8},{10,9... | collective-permute-start | bytes 6152 | tf_op jit(solution)/shard_map/ppermute | solution.py:50
  27.7 11.8 %collective-permute-start.2 = (f32[2,256]{1,0:T(2,128)S(1)}, f32[2,256]{1,0:T(2,128)S(1)}, u32[]{:S(2)}, u32[]{:S(2)}) collective-permute-start(f32[2,256]{1,0:T(2,128)S(1)} %multiply_reduce_fusion), channel_id=1, source_target_pairs={{0,2},{1,3},{2,0},{3,1},{4,6},{5,7},{6,4},{7,5},{8,10},{9,11},{10,... | collective-permute-start | bytes 6152 | tf_op jit(solution)/shard_map/ppermute | solution.py:50
  35.1 13.8 %collective-permute-start.6 = (bf16[256,256]{1,0:T(8,128)(2,1)}, bf16[256,256]{1,0:T(8,128)(2,1)S(1)}, u32[]{:S(2)}, u32[]{:S(2)}) collective-permute-start(bf16[256,256]{1,0:T(8,128)(2,1)} %get-tuple-element.53), channel_id=1, source_target_pairs={{0,0},{1,64},{2,128},{3,192},{4,4},{5,68},{6,132},{7,196},{8,8},{9... | collective-permute-start | bytes 393224 | tf_op jit(solution)/shard_map/ppermute | solution.py:50
  63.7 39.4 %all-to-all-start.1 = ((bf16[16,256,256]{2,1,0:T(8,128)(2,1)}), bf16[16,256,256]{2,1,0:T(8,128)(2,1)}, u32[]{:S(2)}, u32[]{:S(2)}) async-start(bf16[16,256,256]{2,1,0:T(8,128)(2,1)} %broadcast_in_dim.15), calls=%async_computation.1 | async-start | bytes 4194304 | tf_op jit(solution)/shard_map/all_to_all | solution.py:378
  72.3 13.7 %collective-permute-start.8 = (f32[256,256]{1,0:T(8,128)}, f32[256,256]{1,0:T(8,128)S(1)}, u32[]{:S(2)}, u32[]{:S(2)}) collective-permute-start(f32[256,256]{1,0:T(8,128)} %copy-done.33), channel_id=1, source_target_pairs={{0,1},{1,2},{2,3},{3,0},{4,5},{5,6},{6,7},{7,4},{8,9},{9,10},{10,1... | collective-permute-start | bytes 786440 | tf_op jit(solution)/shard_map/ppermute | solution.py:50
  76.7 24.7 %collective-permute-start.9 = (f32[256,256]{1,0:T(8,128)}, f32[256,256]{1,0:T(8,128)S(1)}, u32[]{:S(2)}, u32[]{:S(2)}) collective-permute-start(f32[256,256]{1,0:T(8,128)} %copy-done.32), channel_id=1, source_target_pairs={{0,2},{1,3},{2,0},{3,1},{4,6},{5,7},{6,4},{7,5},{8,10},{9,11},{10,... | collective-permute-start | bytes 786440 | tf_op jit(solution)/shard_map/ppermute | solution.py:50
  78.6 23.7 %collective-permute-start.10 = (f32[256,256]{1,0:T(8,128)}, f32[256,256]{1,0:T(8,128)S(1)}, u32[]{:S(2)}, u32[]{:S(2)}) collective-permute-start(f32[256,256]{1,0:T(8,128)} %copy-done.31), channel_id=1, source_target_pairs={{0,3},{1,0},{2,1},{3,2},{4,7},{5,4},{6,5},{7,6},{8,11},{9,8},{10,9... | collective-permute-start | bytes 786440 | tf_op jit(solution)/shard_map/ppermute | solution.py:50
  113.6 13.3 %collective-permute-start.12 = (f32[256,256]{1,0:T(8,128)S(1)}, f32[256,256]{1,0:T(8,128)S(1)}, u32[]{:S(2)}, u32[]{:S(2)}) collective-permute-start(f32[256,256]{1,0:T(8,128)S(1)} %get-tuple-element.67), channel_id=1, source_target_pairs={{0,1},{1,2},{2,3},{3,0},{4,5},{5,6},{6,7},{7,4},{8,9},{9,10},{10,1... | collective-permute-start | bytes 786440 | tf_op jit(solution)/shard_map/ppermute | solution.py:50
  116.7 25.9 %collective-permute-start.13 = (f32[256,256]{1,0:T(8,128)S(1)}, f32[256,256]{1,0:T(8,128)S(1)}, u32[]{:S(2)}, u32[]{:S(2)}) collective-permute-start(f32[256,256]{1,0:T(8,128)S(1)} %get-tuple-element.68), channel_id=1, source_target_pairs={{0,2},{1,3},{2,0},{3,1},{4,6},{5,7},{6,4},{7,5},{8,10},{9,11},{10,... | collective-permute-start | bytes 786440 | tf_op jit(solution)/shard_map/ppermute | solution.py:50
  119.2 23.7 %collective-permute-start.14 = (f32[256,256]{1,0:T(8,128)S(1)}, f32[256,256]{1,0:T(8,128)S(1)}, u32[]{:S(2)}, u32[]{:S(2)}) collective-permute-start(f32[256,256]{1,0:T(8,128)S(1)} %get-tuple-element.69), channel_id=1, source_target_pairs={{0,3},{1,0},{2,1},{3,2},{4,7},{5,4},{6,5},{7,6},{8,11},{9,8},{10,9... | collective-permute-start | bytes 786440 | tf_op jit(solution)/shard_map/ppermute | solution.py:50
  142.9 13.2 %collective-permute-start.17 = (bf16[272,256]{1,0:T(8,128)(2,1)S(1)}, bf16[272,256]{1,0:T(8,128)(2,1)S(1)}, u32[]{:S(2)}, u32[]{:S(2)}) collective-permute-start(bf16[272,256]{1,0:T(8,128)(2,1)S(1)} %get-tuple-element.78), channel_id=1, source_target_pairs={{0,1},{1,2},{2,3},{3,0},{4,5},{5,6},{6,7},{7,4},{8,9},{9,10},{10,1... | collective-permute-start | bytes 417800 | tf_op jit(solution)/shard_map/ppermute | solution.py:50
  145.4 10.8 %collective-permute-start.16 = (bf16[272,256]{1,0:T(8,128)(2,1)S(1)}, bf16[272,256]{1,0:T(8,128)(2,1)S(1)}, u32[]{:S(2)}, u32[]{:S(2)}) collective-permute-start(bf16[272,256]{1,0:T(8,128)(2,1)S(1)} %get-tuple-element.78), channel_id=1, source_target_pairs={{0,2},{1,3},{2,0},{3,1},{4,6},{5,7},{6,4},{7,5},{8,10},{9,11},{10,... | collective-permute-start | bytes 417800 | tf_op jit(solution)/shard_map/ppermute | solution.py:50
  165.7 35.9 %all-to-all-start.2 = ((bf16[16,256,256]{2,1,0:T(8,128)(2,1)}), bf16[16,256,256]{2,1,0:T(8,128)(2,1)}, u32[]{:S(2)}, u32[]{:S(2)}) async-start(bf16[16,256,256]{2,1,0:T(8,128)(2,1)} %copy-done.9), calls=%async_computation.2 | async-start | bytes 4194304 | tf_op jit(solution)/shard_map/all_to_all | solution.py:378
  176.2 11.2 %collective-permute-start.19 = (bf16[272,256]{1,0:T(8,128)(2,1)S(1)}, bf16[272,256]{1,0:T(8,128)(2,1)S(1)}, u32[]{:S(2)}, u32[]{:S(2)}) collective-permute-start(bf16[272,256]{1,0:T(8,128)(2,1)S(1)} %get-tuple-element.80), channel_id=1, source_target_pairs={{0,2},{1,3},{2,0},{3,1},{4,6},{5,7},{6,4},{7,5},{8,10},{9,11},{10,... | collective-permute-start | bytes 417800 | tf_op jit(solution)/shard_map/ppermute | solution.py:50
  178.5 13.0 %collective-permute-start.18 = (bf16[272,256]{1,0:T(8,128)(2,1)S(1)}, bf16[272,256]{1,0:T(8,128)(2,1)S(1)}, u32[]{:S(2)}, u32[]{:S(2)}) collective-permute-start(bf16[272,256]{1,0:T(8,128)(2,1)S(1)} %get-tuple-element.80), channel_id=1, source_target_pairs={{0,3},{1,0},{2,1},{3,2},{4,7},{5,4},{6,5},{7,6},{8,11},{9,8},{10,9... | collective-permute-start | bytes 417800 | tf_op jit(solution)/shard_map/ppermute | solution.py:50
  201.6 33.9 %all-to-all-start.3 = ((bf16[16,256,256]{2,1,0:T(8,128)(2,1)}), bf16[16,256,256]{2,1,0:T(8,128)(2,1)}, u32[]{:S(2)}, u32[]{:S(2)}) async-start(bf16[16,256,256]{2,1,0:T(8,128)(2,1)} %copy-done.8), calls=%async_computation.3 | async-start | bytes 4194304 | tf_op jit(solution)/shard_map/all_to_all | solution.py:378
  215.9 16.3 %collective-permute-start.24 = (bf16[4,256,256]{2,1,0:T(8,128)(2,1)S(1)}, bf16[4,256,256]{2,1,0:T(8,128)(2,1)S(1)}, u32[]{:S(2)}, u32[]{:S(2)}) collective-permute-start(bf16[4,256,256]{2,1,0:T(8,128)(2,1)S(1)} %get-tuple-element.91), channel_id=1, source_target_pairs={{0,4},{1,5},{2,6},{3,7},{4,0},{5,1},{6,2},{7,3},{8,12},{9,13},{10,... | collective-permute-start | bytes 1572872 | tf_op jit(solution)/shard_map/ppermute | solution.py:50
  222.6 11.2 %collective-permute-start.23 = (bf16[4,256,256]{2,1,0:T(8,128)(2,1)S(1)}, bf16[4,256,256]{2,1,0:T(8,128)(2,1)S(1)}, u32[]{:S(2)}, u32[]{:S(2)}) collective-permute-start(bf16[4,256,256]{2,1,0:T(8,128)(2,1)S(1)} %get-tuple-element.87), channel_id=1, source_target_pairs={{0,4},{1,5},{2,6},{3,7},{4,0},{5,1},{6,2},{7,3},{8,12},{9,13},{10,... | collective-permute-start | bytes 1572872 | tf_op jit(solution)/shard_map/ppermute | solution.py:50
  225.2 17.4 %collective-permute-start.25 = (bf16[256,256]{1,0:T(8,128)(2,1)S(1)}, bf16[256,256]{1,0:T(8,128)(2,1)S(1)}, u32[]{:S(2)}, u32[]{:S(2)}) collective-permute-start(bf16[256,256]{1,0:T(8,128)(2,1)S(1)} %shard_map.91), channel_id=1, source_target_pairs={{0,0},{1,64},{2,128},{3,192},{4,4},{5,68},{6,132},{7,196},{8,8},{9... | collective-permute-start | bytes 393224 | tf_op jit(solution)/shard_map/ppermute | solution.py:50
  237.9 12.1 %collective-permute-start.29 = (bf16[256,256]{1,0:T(8,128)(2,1)S(1)}, bf16[256,256]{1,0:T(8,128)(2,1)S(1)}, u32[]{:S(2)}, u32[]{:S(2)}) collective-permute-start(bf16[256,256]{1,0:T(8,128)(2,1)S(1)} %shard_map.92), channel_id=1, source_target_pairs={{0,0},{1,64},{2,128},{3,192},{4,4},{5,68},{6,132},{7,196},{8,8},{9... | collective-permute-start | bytes 393224 | tf_op jit(solution)/shard_map/ppermute | solution.py:50
  242.6 12.8 %collective-permute-start.28 = (bf16[256,256]{1,0:T(8,128)(2,1)S(1)}, bf16[256,256]{1,0:T(8,128)(2,1)S(1)}, u32[]{:S(2)}, u32[]{:S(2)}) collective-permute-start(bf16[256,256]{1,0:T(8,128)(2,1)S(1)} %collective-permute-done.25.refs_0_), channel_id=1, source_target_pairs={{0,12},{1,13},{2,14},{3,15},{4,8},{5,9},{6,10},{7,11},{8,4},{9,5},... | collective-permute-start | bytes 393224 | tf_op jit(solution)/shard_map/ppermute | solution.py:50
  (47 other events, 187.2 us)

commit v3 on v2

--- a/solution.py
+++ b/solution.py
@@ -396,7 +396,7 @@
     blocks = fetch(sent)
     owned = shift(after(half[1], sent), SWAP)
     sent = jnp.broadcast_to(owned, (16,) + TILE)
-    blocks0 = after(blocks, owned).reshape((4, 4) + TILE)
+    blocks0 = after(blocks, sent).reshape((4, 4) + TILE)
     sums = partial(0, blocks0)
     sent = after(sent, *sums)
     parts = reduce_heads(sums)
@@ -414,14 +414,15 @@
     own0, sib0 = after((own0, sib0), terms0)
     terms0 = fetch(terms0)
 
-    own1 = gather_heads(joined)
+    own1 = lax.all_gather(joined, "tensor", axis=0)
+    in_order = where.at[3].set(0)
     sib1 = shift(own1, CORE)
-    terms1 = slab_terms(1, where, turned, own1, sib1)
+    terms1 = slab_terms(1, in_order, turned, own1, sib1)
     own1, sib1, own0 = after((own1, sib1, own0), terms1)
     terms1 = fetch(terms1)
     own_out, sib_out = spread_out(0, where, states, own0, sib0, blocks0)
     hidden_grads = unsplit(0, where, own_out, shift(sib_out, CORE), hidden.shape, [])
-    own_out, sib_out = spread_out(1, where, states, own1, sib1, blocks1)
+    own_out, sib_out = spread_out(1, in_order, states, own1, sib1, blocks1)
     hidden_grads = unsplit(1, where, own_out, shift(sib_out, CORE), hidden.shape, [hidden_grads])
 
     total = after(plane_total(terms0), own_out)

time: 267 us -> 265 us (level)
  blocking collectives: 0 us -> 16.8 us
  waiting for transfers between devices: 63.3 us -> 53.5 us
  starting transfers between devices: 116 us -> 110 us
    all_gather x0 -> x1, blocking collectives: none -> 16.8 us  [shards(): own1 = lax.all_gather(joined, 'tensor', axis=0)]
    ppermute x33 -> x30, waiting for transfers between devices: 61 us -> 50.6 us  [shift(): return lax.ppermute(value, AXES, pairs)]
    ppermute x33 -> x30, starting transfers between devices: 84.1 us -> 78 us  [shift(): return lax.ppermute(value, AXES, pairs)]
    unnamed x68 -> x69, local copies, waits for them, and re-layouts: 25.2 us -> 24.4 us
  transfers between devices with their start and end apart: 37 -> 34, of which waited for: 19 -> 16; matrix products, arithmetic and copies ran while one was open for 1% -> 1% of each run, Pallas kernels for 15% -> 15%
where the time goes in v3:
time: 265 us; the launch traced here: 262 us
  starting transfers between devices  110 us (42%)
  waiting for transfers between devices  53.5 us (20%)
  Pallas kernels  49.9 us (19%)
  local copies, waits for them, and re-layouts  30.3 us (11%)
  blocking collectives  16.8 us (6%)
    ppermute x30, starting transfers between devices, shift(): return lax.ppermute(value, AXES, pairs)  78 us
    ppermute x30, waiting for transfers between devices, shift(): return lax.ppermute(value, AXES, pairs)  50.6 us
    pallas_call x19, Pallas kernels, run(): pl.pallas_call(kernel, out_shape=outs, grid_spec=pltpu.PrefetchScalarGrid...  49.9 us
    all_to_all x4, starting transfers between devices, fetch(): return lax.all_to_all(sent, 'layer', 0, 0, tiled=True)  32.5 us
    unnamed x69, local copies, waits for them, and re-layouts  24.4 us
    all_gather x1, blocking collectives, shards(): own1 = lax.all_gather(joined, 'tensor', axis=0)  16.8 us
  transfers between devices with their start and end apart: 34, of which 16 were waited for; matrix products, arithmetic and copies ran while one was open for 1% of the time, Pallas kernels for 15%

profile of v3, /device:TPU:71, one launch (start us, length us, event | category | flops | bytes accessed | tf_op | source)
XLA Modules:
  0.0 262.5 jit_solution(11319289642575120280)
XLA Ops:
  2.3 7.8 %collective-permute-start.5 = (bf16[256,256]{1,0:T(8,128)(2,1)S(1)}, bf16[256,256]{1,0:T(8,128)(2,1)S(1)}, u32[]{:S(2)}, u32[]{:S(2)}) collective-permute-start(bf16[256,256]{1,0:T(8,128)(2,1)S(1)} %get-tuple-element.107), channel_id=1, source_target_pairs={{0,0},{1,64},{2,128},{3,192},{4,4},{5,68},{6,132},{7,196},{8,8},{9... | collective-permute-start | bytes 393224 | tf_op jit(solution)/shard_map/ppermute | solution.py:50
  16.4 9.2 %all-to-all-start = ((bf16[16,256,256]{2,1,0:T(8,128)(2,1)}), bf16[16,256,256]{2,1,0:T(8,128)(2,1)S(1)}, u32[]{:S(2)}, u32[]{:S(2)}) async-start(bf16[16,256,256]{2,1,0:T(8,128)(2,1)} %broadcast_in_dim.14), calls=%async_computation | async-start | bytes 4194304 | tf_op jit(solution)/shard_map/all_to_all | solution.py:378
  27.7 4.8 %collective-permute-start.2 = (f32[2,256]{1,0:T(2,128)S(1)}, f32[2,256]{1,0:T(2,128)S(1)}, u32[]{:S(2)}, u32[]{:S(2)}) collective-permute-start(f32[2,256]{1,0:T(2,128)S(1)} %multiply_reduce_fusion), channel_id=1, source_target_pairs={{0,2},{1,3},{2,0},{3,1},{4,6},{5,7},{6,4},{7,5},{8,10},{9,11},{10,... | collective-permute-start | bytes 6152 | tf_op jit(solution)/shard_map/ppermute | solution.py:50
  35.1 4.3 %collective-permute-start.6 = (bf16[256,256]{1,0:T(8,128)(2,1)}, bf16[256,256]{1,0:T(8,128)(2,1)S(1)}, u32[]{:S(2)}, u32[]{:S(2)}) collective-permute-start(bf16[256,256]{1,0:T(8,128)(2,1)} %get-tuple-element.65), channel_id=1, source_target_pairs={{0,0},{1,64},{2,128},{3,192},{4,4},{5,68},{6,132},{7,196},{8,8},{9... | collective-permute-start | bytes 393224 | tf_op jit(solution)/shard_map/ppermute | solution.py:50
  54.3 3.4 %collective-permute-start.7 = (f32[4,256,256]{2,1,0:T(8,128)S(1)}, f32[4,256,256]{2,1,0:T(8,128)S(1)}, u32[]{:S(2)}, u32[]{:S(2)}) collective-permute-start(f32[4,256,256]{2,1,0:T(8,128)S(1)} %shard_map.78), channel_id=1, source_target_pairs={{0,4},{1,5},{2,6},{3,7},{4,0},{5,1},{6,2},{7,3},{8,12},{9,13},{10,... | collective-permute-start | bytes 3145736 | tf_op jit(solution)/shard_map/ppermute | solution.py:50
  63.0 8.6 %all-to-all-start.1 = ((bf16[16,256,256]{2,1,0:T(8,128)(2,1)}), bf16[16,256,256]{2,1,0:T(8,128)(2,1)}, u32[]{:S(2)}, u32[]{:S(2)}) async-start(bf16[16,256,256]{2,1,0:T(8,128)(2,1)} %broadcast_in_dim.15), calls=%async_computation.1 | async-start | bytes 4194304 | tf_op jit(solution)/shard_map/all_to_all | solution.py:378
  71.5 4.4 %collective-permute-start.8 = (f32[256,256]{1,0:T(8,128)}, f32[256,256]{1,0:T(8,128)S(1)}, u32[]{:S(2)}, u32[]{:S(2)}) collective-permute-start(f32[256,256]{1,0:T(8,128)} %copy-done.33), channel_id=1, source_target_pairs={{0,1},{1,2},{2,3},{3,0},{4,5},{5,6},{6,7},{7,4},{8,9},{9,10},{10,1... | collective-permute-start | bytes 786440 | tf_op jit(solution)/shard_map/ppermute | solution.py:50
  80.2 5.1 %collective-permute-done.8.refs_1_ = f32[256,256]{1,0:T(8,128)S(1)} collective-permute-done((f32[256,256]{1,0:T(8,128)}, f32[256,256]{1,0:T(8,128)S(1)}, u32[]{:S(2)}, u32[]{:S(2)}) %collective-permute-start.8) | collective-permute-done | bytes 262176 | tf_op jit(solution)/shard_map/ppermute | solution.py:50
  85.9 14.7 %collective-permute-done.9.refs_2_ = f32[256,256]{1,0:T(8,128)S(1)} collective-permute-done((f32[256,256]{1,0:T(8,128)}, f32[256,256]{1,0:T(8,128)S(1)}, u32[]{:S(2)}, u32[]{:S(2)}) %collective-permute-start.9) | collective-permute-done | bytes 262176 | tf_op jit(solution)/shard_map/ppermute | solution.py:50
  103.9 3.6 %shard_map.82 = f32[4,256,256]{2,1,0:T(8,128)S(1)} custom-call(s32[5]{0:T(128)S(1)} %stack.38.where, bf16[2,2,4,256,256]{4,3,2,1,0:T(8,128)(2,1)S(1)} %copy-done.2, bf16[4,4,256,256]{3,2,1,0:T(8,128)(2,1)} %bitcast.10.blocks), custom_call_target="tpu_custom_call" | custom-call | flops 537000000 | bytes 6291456 | tf_op jit(solution)/shard_map/pallas_call | solution.py:212
  109.1 3.6 %shard_map.81.own = f32[4,256,256]{2,1,0:T(8,128)S(1)} custom-call(s32[5]{0:T(128)S(1)} %stack.38.where, bf16[2,2,4,256,256]{4,3,2,1,0:T(8,128)(2,1)S(1)} %copy-done.2, bf16[4,4,256,256]{3,2,1,0:T(8,128)(2,1)} %bitcast.10.blocks), custom_call_target="tpu_custom_call" | custom-call | flops 537000000 | bytes 6291456 | tf_op jit(solution)/shard_map/pallas_call | solution.py:212
  120.6 5.6 %shard_map.80 = (bf16[2,256,1024]{2,1,0:T(8,128)(2,1)}, bf16[2,256,1024]{2,1,0:T(8,128)(2,1)}, bf16[272,256]{1,0:T(8,128)(2,1)S(1)}) custom-call(f32[256,256]{1,0:T(8,128)S(1)} %copy-done.24, f32[256,256]{1,0:T(8,128)S(1)} %copy-done.26, f32[256,256]{1,0:T(8,128)S(1)} %copy-done.28, f32[256,256]{1,0:T(8,128)S(1)} %copy-done.30, ...), custom_call_target="tpu_custom_call" | custom-call | flops 5000000000 | bytes 6291456 | tf_op jit(solution)/shard_map/pallas_call | solution.py:212
  126.2 15.6 %collective-permute-done.13.refs_2_ = f32[256,256]{1,0:T(8,128)S(1)} collective-permute-done((f32[256,256]{1,0:T(8,128)S(1)}, f32[256,256]{1,0:T(8,128)S(1)}, u32[]{:S(2)}, u32[]{:S(2)}) %collective-permute-start.13) | collective-permute-done | bytes 262176 | tf_op jit(solution)/shard_map/ppermute | solution.py:50
  149.8 5.6 %shard_map.84 = (bf16[2,256,1024]{2,1,0:T(8,128)(2,1)}, bf16[2,256,1024]{2,1,0:T(8,128)(2,1)}, bf16[272,256]{1,0:T(8,128)(2,1)S(1)}) custom-call(f32[256,256]{1,0:T(8,128)S(1)} %get-tuple-element.82.refs_0_, f32[256,256]{1,0:T(8,128)S(1)} %collective-permute-done.12.refs_1_, ...), custom_call_target="tpu_custom_call", output_to_operand_aliasing={{0}: (6, {}), {1}: (7, {})} | custom-call | flops 5000000000 | bytes 6291456 | tf_op jit(solution)/shard_map/pallas_call | solution.py:212
  165.0 7.9 %all-to-all-start.2 = ((bf16[16,256,256]{2,1,0:T(8,128)(2,1)}), bf16[16,256,256]{2,1,0:T(8,128)(2,1)}, u32[]{:S(2)}, u32[]{:S(2)}) async-start(bf16[16,256,256]{2,1,0:T(8,128)(2,1)} %copy-done.9), calls=%async_computation.2 | async-start | bytes 4194304 | tf_op jit(solution)/shard_map/all_to_all | solution.py:378
  172.8 16.8 %all-gather = bf16[1088,256]{1,0:T(8,128)(2,1)S(1)} all-gather(bf16[272,256]{1,0:T(8,128)(2,1)S(1)} %get-tuple-element.92), channel_id=2, replica_groups=mesh['layer'=16,'dp'=4,'tensor'=4] {'tensor'}, dimensions={0}, use_global_device_ids=true | all-gather | bytes 696320 | tf_op jit(solution)/shard_map/all_gather | solution.py:417
  200.7 6.9 %all-to-all-start.3 = ((bf16[16,256,256]{2,1,0:T(8,128)(2,1)}), bf16[16,256,256]{2,1,0:T(8,128)(2,1)}, u32[]{:S(2)}, u32[]{:S(2)}) async-start(bf16[16,256,256]{2,1,0:T(8,128)(2,1)} %copy-done.8), calls=%async_computation.3 | async-start | bytes 4194304 | tf_op jit(solution)/shard_map/all_to_all | solution.py:378
  210.6 4.4 %shard_map.88 = (bf16[4,256,256]{2,1,0:T(8,128)(2,1)S(1)}, bf16[4,256,256]{2,1,0:T(8,128)(2,1)S(1)}) custom-call(s32[5]{0:T(128)S(1)} %stack.38.where, bf16[2,4,256,256]{3,2,1,0:T(8,128)(2,1)S(1)} %get-tuple-element.61.keep, bf16[2,4,256,256]{3,2,1,0:T(8,128)(2,1)} %collective-permute-done.sib, f32[2,256,1]{2,1,0:T(8,128)S(1)} %copy.17.inverse, ...), custom_call_target="tpu_custom_call" | custom-call | flops 1074000000 | bytes 6291456 | tf_op jit(solution)/shard_map/pallas_call | solution.py:212
  217.0 4.9 %shard_map.87 = (bf16[4,256,256]{2,1,0:T(8,128)(2,1)S(1)}, bf16[4,256,256]{2,1,0:T(8,128)(2,1)S(1)}) custom-call(s32[5]{0:T(128)S(1)} %constant_dynamic-update-slice_fusion.where, bf16[2,4,256,256]{3,2,1,0:T(8,128)(2,1)S(1)} %get-tuple-element.61.keep, bf16[2,4,256,256]{3,2,1,0:T(8,128)(2,1)} %collective-permute-done.sib, f32[2,256,1]{2,1,0:T(8,128)S(1)} %copy.17.inverse, ...), custom_call_target="tpu_custom_call" | custom-call | flops 1074000000 | bytes 6291456 | tf_op jit(solution)/shard_map/pallas_call | solution.py:212
  224.5 6.9 %collective-permute-start.22 = (bf16[256,256]{1,0:T(8,128)(2,1)S(1)}, bf16[256,256]{1,0:T(8,128)(2,1)S(1)}, u32[]{:S(2)}, u32[]{:S(2)}) collective-permute-start(bf16[256,256]{1,0:T(8,128)(2,1)S(1)} %shard_map.91), channel_id=1, source_target_pairs={{0,0},{1,64},{2,128},{3,192},{4,4},{5,68},{6,132},{7,196},{8,8},{9... | collective-permute-start | bytes 393224 | tf_op jit(solution)/shard_map/ppermute | solution.py:50
  237.2 4.7 %collective-permute-start.26 = (bf16[256,256]{1,0:T(8,128)(2,1)S(1)}, bf16[256,256]{1,0:T(8,128)(2,1)S(1)}, u32[]{:S(2)}, u32[]{:S(2)}) collective-permute-start(bf16[256,256]{1,0:T(8,128)(2,1)S(1)} %shard_map.92), channel_id=1, source_target_pairs={{0,0},{1,64},{2,128},{3,192},{4,4},{5,68},{6,132},{7,196},{8,8},{9... | collective-permute-start | bytes 393224 | tf_op jit(solution)/shard_map/ppermute | solution.py:50
  241.8 3.3 %collective-permute-start.25 = (bf16[256,256]{1,0:T(8,128)(2,1)S(1)}, bf16[256,256]{1,0:T(8,128)(2,1)S(1)}, u32[]{:S(2)}, u32[]{:S(2)}) collective-permute-start(bf16[256,256]{1,0:T(8,128)(2,1)S(1)} %collective-permute-done.22.refs_0_), channel_id=1, source_target_pairs={{0,12},{1,13},{2,14},{3,15},{4,8},{5,9},{6,10},{7,11},{8,4},{9,5},... | collective-permute-start | bytes 393224 | tf_op jit(solution)/shard_map/ppermute | solution.py:50
  249.3 4.9 %collective-permute-start.29 = (bf16[256,256]{1,0:T(8,128)(2,1)S(1)}, bf16[256,256]{1,0:T(8,128)(2,1)S(1)}, u32[]{:S(2)}, u32[]{:S(2)}) collective-permute-start(bf16[256,256]{1,0:T(8,128)(2,1)S(1)} %collective-permute-done.26.refs_4_), channel_id=1, source_target_pairs={{0,12},{1,13},{2,14},{3,15},{4,8},{5,9},{6,10},{7,11},{8,4},{9,5},... | collective-permute-start | bytes 393224 | tf_op jit(solution)/shard_map/ppermute | solution.py:50
  254.6 3.6 %collective-permute-done.29.refs_7_ = bf16[256,256]{1,0:T(8,128)(2,1)S(1)} collective-permute-done((bf16[256,256]{1,0:T(8,128)(2,1)S(1)}, bf16[256,256]{1,0:T(8,128)(2,1)S(1)}, u32[]{:S(2)}, u32[]{:S(2)}) %collective-permute-start.29) | collective-permute-done | bytes 131104 | tf_op jit(solution)/shard_map/ppermute | solution.py:50
  (143 shorter events, 100.8 us)
Async XLA Ops:
  2.3 12.6 %collective-permute-start.5 = (bf16[256,256]{1,0:T(8,128)(2,1)S(1)}, bf16[256,256]{1,0:T(8,128)(2,1)S(1)}, u32[]{:S(2)}, u32[]{:S(2)}) collective-permute-start(bf16[256,256]{1,0:T(8,128)(2,1)S(1)} %get-tuple-element.107), channel_id=1, source_target_pairs={{0,0},{1,64},{2,128},{3,192},{4,4},{5,68},{6,132},{7,196},{8,8},{9... | collective-permute-start | bytes 393224 | tf_op jit(solution)/shard_map/ppermute | solution.py:50
  16.4 33.8 %all-to-all-start = ((bf16[16,256,256]{2,1,0:T(8,128)(2,1)}), bf16[16,256,256]{2,1,0:T(8,128)(2,1)S(1)}, u32[]{:S(2)}, u32[]{:S(2)}) async-start(bf16[16,256,256]{2,1,0:T(8,128)(2,1)} %broadcast_in_dim.14), calls=%async_computation | async-start | bytes 4194304 | tf_op jit(solution)/shard_map/all_to_all | solution.py:378
  25.6 16.9 %collective-permute-start = (bf16[2,4,256,256]{3,2,1,0:T(8,128)(2,1)}, bf16[2,4,256,256]{3,2,1,0:T(8,128)(2,1)}, u32[]{:S(2)}, u32[]{:S(2)}) collective-permute-start(bf16[2,4,256,256]{3,2,1,0:T(8,128)(2,1)} %copy-done.22), channel_id=1, source_target_pairs={{0,4},{1,5},{2,6},{3,7},{4,0},{5,1},{6,2},{7,3},{8,12},{9,13},{10,... | collective-permute-start | bytes 3145736 | tf_op jit(solution)/shard_map/ppermute | solution.py:50
  27.7 11.8 %collective-permute-start.3 = (f32[2,256]{1,0:T(2,128)S(1)}, f32[2,256]{1,0:T(2,128)S(1)}, u32[]{:S(2)}, u32[]{:S(2)}) collective-permute-start(f32[2,256]{1,0:T(2,128)S(1)} %multiply_reduce_fusion), channel_id=1, source_target_pairs={{0,3},{1,0},{2,1},{3,2},{4,7},{5,4},{6,5},{7,6},{8,11},{9,8},{10,9... | collective-permute-start | bytes 6152 | tf_op jit(solution)/shard_map/ppermute | solution.py:50
  27.7 11.8 %collective-permute-start.2 = (f32[2,256]{1,0:T(2,128)S(1)}, f32[2,256]{1,0:T(2,128)S(1)}, u32[]{:S(2)}, u32[]{:S(2)}) collective-permute-start(f32[2,256]{1,0:T(2,128)S(1)} %multiply_reduce_fusion), channel_id=1, source_target_pairs={{0,2},{1,3},{2,0},{3,1},{4,6},{5,7},{6,4},{7,5},{8,10},{9,11},{10,... | collective-permute-start | bytes 6152 | tf_op jit(solution)/shard_map/ppermute | solution.py:50
  35.1 13.8 %collective-permute-start.6 = (bf16[256,256]{1,0:T(8,128)(2,1)}, bf16[256,256]{1,0:T(8,128)(2,1)S(1)}, u32[]{:S(2)}, u32[]{:S(2)}) collective-permute-start(bf16[256,256]{1,0:T(8,128)(2,1)} %get-tuple-element.65), channel_id=1, source_target_pairs={{0,0},{1,64},{2,128},{3,192},{4,4},{5,68},{6,132},{7,196},{8,8},{9... | collective-permute-start | bytes 393224 | tf_op jit(solution)/shard_map/ppermute | solution.py:50
  63.0 39.4 %all-to-all-start.1 = ((bf16[16,256,256]{2,1,0:T(8,128)(2,1)}), bf16[16,256,256]{2,1,0:T(8,128)(2,1)}, u32[]{:S(2)}, u32[]{:S(2)}) async-start(bf16[16,256,256]{2,1,0:T(8,128)(2,1)} %broadcast_in_dim.15), calls=%async_computation.1 | async-start | bytes 4194304 | tf_op jit(solution)/shard_map/all_to_all | solution.py:378
  71.5 13.7 %collective-permute-start.8 = (f32[256,256]{1,0:T(8,128)}, f32[256,256]{1,0:T(8,128)S(1)}, u32[]{:S(2)}, u32[]{:S(2)}) collective-permute-start(f32[256,256]{1,0:T(8,128)} %copy-done.33), channel_id=1, source_target_pairs={{0,1},{1,2},{2,3},{3,0},{4,5},{5,6},{6,7},{7,4},{8,9},{9,10},{10,1... | collective-permute-start | bytes 786440 | tf_op jit(solution)/shard_map/ppermute | solution.py:50
  76.0 24.7 %collective-permute-start.9 = (f32[256,256]{1,0:T(8,128)}, f32[256,256]{1,0:T(8,128)S(1)}, u32[]{:S(2)}, u32[]{:S(2)}) collective-permute-start(f32[256,256]{1,0:T(8,128)} %copy-done.32), channel_id=1, source_target_pairs={{0,2},{1,3},{2,0},{3,1},{4,6},{5,7},{6,4},{7,5},{8,10},{9,11},{10,... | collective-permute-start | bytes 786440 | tf_op jit(solution)/shard_map/ppermute | solution.py:50
  77.9 23.7 %collective-permute-start.10 = (f32[256,256]{1,0:T(8,128)}, f32[256,256]{1,0:T(8,128)S(1)}, u32[]{:S(2)}, u32[]{:S(2)}) collective-permute-start(f32[256,256]{1,0:T(8,128)} %copy-done.31), channel_id=1, source_target_pairs={{0,3},{1,0},{2,1},{3,2},{4,7},{5,4},{6,5},{7,6},{8,11},{9,8},{10,9... | collective-permute-start | bytes 786440 | tf_op jit(solution)/shard_map/ppermute | solution.py:50
  112.9 13.3 %collective-permute-start.12 = (f32[256,256]{1,0:T(8,128)S(1)}, f32[256,256]{1,0:T(8,128)S(1)}, u32[]{:S(2)}, u32[]{:S(2)}) collective-permute-start(f32[256,256]{1,0:T(8,128)S(1)} %get-tuple-element.79), channel_id=1, source_target_pairs={{0,1},{1,2},{2,3},{3,0},{4,5},{5,6},{6,7},{7,4},{8,9},{9,10},{10,1... | collective-permute-start | bytes 786440 | tf_op jit(solution)/shard_map/ppermute | solution.py:50
  115.9 25.9 %collective-permute-start.13 = (f32[256,256]{1,0:T(8,128)S(1)}, f32[256,256]{1,0:T(8,128)S(1)}, u32[]{:S(2)}, u32[]{:S(2)}) collective-permute-start(f32[256,256]{1,0:T(8,128)S(1)} %get-tuple-element.80), channel_id=1, source_target_pairs={{0,2},{1,3},{2,0},{3,1},{4,6},{5,7},{6,4},{7,5},{8,10},{9,11},{10,... | collective-permute-start | bytes 786440 | tf_op jit(solution)/shard_map/ppermute | solution.py:50
  118.5 23.7 %collective-permute-start.14 = (f32[256,256]{1,0:T(8,128)S(1)}, f32[256,256]{1,0:T(8,128)S(1)}, u32[]{:S(2)}, u32[]{:S(2)}) collective-permute-start(f32[256,256]{1,0:T(8,128)S(1)} %get-tuple-element.81), channel_id=1, source_target_pairs={{0,3},{1,0},{2,1},{3,2},{4,7},{5,4},{6,5},{7,6},{8,11},{9,8},{10,9... | collective-permute-start | bytes 786440 | tf_op jit(solution)/shard_map/ppermute | solution.py:50
  142.2 13.2 %collective-permute-start.17 = (bf16[272,256]{1,0:T(8,128)(2,1)S(1)}, bf16[272,256]{1,0:T(8,128)(2,1)S(1)}, u32[]{:S(2)}, u32[]{:S(2)}) collective-permute-start(bf16[272,256]{1,0:T(8,128)(2,1)S(1)} %get-tuple-element.90), channel_id=1, source_target_pairs={{0,1},{1,2},{2,3},{3,0},{4,5},{5,6},{6,7},{7,4},{8,9},{9,10},{10,1... | collective-permute-start | bytes 417800 | tf_op jit(solution)/shard_map/ppermute | solution.py:50
  144.6 10.8 %collective-permute-start.16 = (bf16[272,256]{1,0:T(8,128)(2,1)S(1)}, bf16[272,256]{1,0:T(8,128)(2,1)S(1)}, u32[]{:S(2)}, u32[]{:S(2)}) collective-permute-start(bf16[272,256]{1,0:T(8,128)(2,1)S(1)} %get-tuple-element.90), channel_id=1, source_target_pairs={{0,2},{1,3},{2,0},{3,1},{4,6},{5,7},{6,4},{7,5},{8,10},{9,11},{10,... | collective-permute-start | bytes 417800 | tf_op jit(solution)/shard_map/ppermute | solution.py:50
  147.6 9.3 %collective-permute-start.15 = (bf16[272,256]{1,0:T(8,128)(2,1)S(1)}, bf16[272,256]{1,0:T(8,128)(2,1)S(1)}, u32[]{:S(2)}, u32[]{:S(2)}) collective-permute-start(bf16[272,256]{1,0:T(8,128)(2,1)S(1)} %get-tuple-element.90), channel_id=1, source_target_pairs={{0,3},{1,0},{2,1},{3,2},{4,7},{5,4},{6,5},{7,6},{8,11},{9,8},{10,9... | collective-permute-start | bytes 417800 | tf_op jit(solution)/shard_map/ppermute | solution.py:50
  165.0 35.8 %all-to-all-start.2 = ((bf16[16,256,256]{2,1,0:T(8,128)(2,1)}), bf16[16,256,256]{2,1,0:T(8,128)(2,1)}, u32[]{:S(2)}, u32[]{:S(2)}) async-start(bf16[16,256,256]{2,1,0:T(8,128)(2,1)} %copy-done.9), calls=%async_computation.2 | async-start | bytes 4194304 | tf_op jit(solution)/shard_map/all_to_all | solution.py:378
  200.7 34.0 %all-to-all-start.3 = ((bf16[16,256,256]{2,1,0:T(8,128)(2,1)}), bf16[16,256,256]{2,1,0:T(8,128)(2,1)}, u32[]{:S(2)}, u32[]{:S(2)}) async-start(bf16[16,256,256]{2,1,0:T(8,128)(2,1)} %copy-done.8), calls=%async_computation.3 | async-start | bytes 4194304 | tf_op jit(solution)/shard_map/all_to_all | solution.py:378
  215.1 16.3 %collective-permute-start.21 = (bf16[4,256,256]{2,1,0:T(8,128)(2,1)S(1)}, bf16[4,256,256]{2,1,0:T(8,128)(2,1)S(1)}, u32[]{:S(2)}, u32[]{:S(2)}) collective-permute-start(bf16[4,256,256]{2,1,0:T(8,128)(2,1)S(1)} %get-tuple-element.103), channel_id=1, source_target_pairs={{0,4},{1,5},{2,6},{3,7},{4,0},{5,1},{6,2},{7,3},{8,12},{9,13},{10,... | collective-permute-start | bytes 1572872 | tf_op jit(solution)/shard_map/ppermute | solution.py:50
  221.9 11.2 %collective-permute-start.20 = (bf16[4,256,256]{2,1,0:T(8,128)(2,1)S(1)}, bf16[4,256,256]{2,1,0:T(8,128)(2,1)S(1)}, u32[]{:S(2)}, u32[]{:S(2)}) collective-permute-start(bf16[4,256,256]{2,1,0:T(8,128)(2,1)S(1)} %get-tuple-element.99), channel_id=1, source_target_pairs={{0,4},{1,5},{2,6},{3,7},{4,0},{5,1},{6,2},{7,3},{8,12},{9,13},{10,... | collective-permute-start | bytes 1572872 | tf_op jit(solution)/shard_map/ppermute | solution.py:50
  224.5 17.4 %collective-permute-start.22 = (bf16[256,256]{1,0:T(8,128)(2,1)S(1)}, bf16[256,256]{1,0:T(8,128)(2,1)S(1)}, u32[]{:S(2)}, u32[]{:S(2)}) collective-permute-start(bf16[256,256]{1,0:T(8,128)(2,1)S(1)} %shard_map.91), channel_id=1, source_target_pairs={{0,0},{1,64},{2,128},{3,192},{4,4},{5,68},{6,132},{7,196},{8,8},{9... | collective-permute-start | bytes 393224 | tf_op jit(solution)/shard_map/ppermute | solution.py:50
  237.2 12.1 %collective-permute-start.26 = (bf16[256,256]{1,0:T(8,128)(2,1)S(1)}, bf16[256,256]{1,0:T(8,128)(2,1)S(1)}, u32[]{:S(2)}, u32[]{:S(2)}) collective-permute-start(bf16[256,256]{1,0:T(8,128)(2,1)S(1)} %shard_map.92), channel_id=1, source_target_pairs={{0,0},{1,64},{2,128},{3,192},{4,4},{5,68},{6,132},{7,196},{8,8},{9... | collective-permute-start | bytes 393224 | tf_op jit(solution)/shard_map/ppermute | solution.py:50
  241.8 12.4 %collective-permute-start.25 = (bf16[256,256]{1,0:T(8,128)(2,1)S(1)}, bf16[256,256]{1,0:T(8,128)(2,1)S(1)}, u32[]{:S(2)}, u32[]{:S(2)}) collective-permute-start(bf16[256,256]{1,0:T(8,128)(2,1)S(1)} %collective-permute-done.22.refs_0_), channel_id=1, source_target_pairs={{0,12},{1,13},{2,14},{3,15},{4,8},{5,9},{6,10},{7,11},{8,4},{9,5},... | collective-permute-start | bytes 393224 | tf_op jit(solution)/shard_map/ppermute | solution.py:50
  245.1 9.5 %collective-permute-start.24 = (bf16[256,256]{1,0:T(8,128)(2,1)S(1)}, bf16[256,256]{1,0:T(8,128)(2,1)S(1)}, u32[]{:S(2)}, u32[]{:S(2)}) collective-permute-start(bf16[256,256]{1,0:T(8,128)(2,1)S(1)} %collective-permute-done.22.refs_0_), channel_id=1, source_target_pairs={{0,8},{1,9},{2,10},{3,11},{4,12},{5,13},{6,14},{7,15},{8,0},{9,1},... | collective-permute-start | bytes 393224 | tf_op jit(solution)/shard_map/ppermute | solution.py:50
  (44 other events, 165.8 us)

commit v4 on v3

--- a/solution.py
+++ b/solution.py
@@ -385,10 +385,6 @@
         arrived = {k: shift(sums[k], along_high(k)) for k in STEPS}
         return [sums[0]] + [arrived[k] for k in (1, 2, 3)]
 
-    def gather_heads(joined):
-        arrived = {k: shift(joined, along_high(-k)) for k in STEPS}
-        return jnp.stack([joined] + [arrived[k] for k in (1, 2, 3)])
-
     def spread(placed):
         return [placed] + [shift(placed, pairs) for pairs in (CORE, LOW, BOTH)]
 
@@ -406,21 +402,20 @@
     sums = partial(1, blocks1)
 
     joined, parts = lax.optimization_barrier((joined, reduce_heads(sums)))
-    own0 = gather_heads(joined)
+    own0 = lax.all_gather(joined, "tensor", axis=0)
+    in_order = where.at[3].set(0)
+    sib0 = shift(own0, CORE)
+    terms0 = slab_terms(0, in_order, turned, own0, sib0)
+    own0, sib0, parts = after((own0, sib0, parts), terms0)
+    terms0 = fetch(terms0)
     attended, query_grads, joined = attend(1, parts, queries, cotangent, [attended, query_grads])
-    own0, joined = lax.optimization_barrier((own0, joined))
-    sib0 = shift(own0, CORE)
-    terms0 = slab_terms(0, where, turned, own0, sib0)
-    own0, sib0 = after((own0, sib0), terms0)
-    terms0 = fetch(terms0)
 
     own1 = lax.all_gather(joined, "tensor", axis=0)
-    in_order = where.at[3].set(0)
     sib1 = shift(own1, CORE)
     terms1 = slab_terms(1, in_order, turned, own1, sib1)
     own1, sib1, own0 = after((own1, sib1, own0), terms1)
     terms1 = fetch(terms1)
-    own_out, sib_out = spread_out(0, where, states, own0, sib0, blocks0)
+    own_out, sib_out = spread_out(0, in_order, states, own0, sib0, blocks0)
     hidden_grads = unsplit(0, where, own_out, shift(sib_out, CORE), hidden.shape, [])
     own_out, sib_out = spread_out(1, in_order, states, own1, sib1, blocks1)
     hidden_grads = unsplit(1, where, own_out, shift(sib_out, CORE), hidden.shape, [hidden_grads])

time: 265 us -> 279 us (1.053)
  blocking collectives: 16.8 us -> 29.6 us
  local copies, waits for them, and re-layouts: 30.3 us -> 36.3 us
  starting transfers between devices: 110 us -> 107 us
    all_gather x0 -> x1, blocking collectives: none -> 15.7 us  [shards(): own0 = lax.all_gather(joined, 'tensor', axis=0)]
    unnamed x69 -> x89, local copies, waits for them, and re-layouts: 24.4 us -> 30.4 us
    all_gather x1, blocking collectives: 16.8 us -> 13.9 us  [shards(): own1 = lax.all_gather(joined, 'tensor', axis=0)]
    ppermute x30 -> x27, starting transfers between devices: 78 us -> 76.1 us  [shift(): return lax.ppermute(value, AXES, pairs)]
    ppermute x30 -> x27, waiting for transfers between devices: 50.6 us -> 48.9 us  [shift(): return lax.ppermute(value, AXES, pairs)]
  transfers between devices with their start and end apart: 34 -> 31, of which waited for: 16 -> 14; matrix products, arithmetic and copies ran while one was open for 1% -> 1% of each run, Pallas kernels for 15% -> 15%
where the time goes in v4:
time: 279 us; the launch traced here: 276 us
  starting transfers between devices  107 us (38%)
  waiting for transfers between devices  52.1 us (19%)
  Pallas kernels  49.9 us (18%)
  local copies, waits for them, and re-layouts  36.3 us (13%)
  blocking collectives  29.6 us (11%)
    ppermute x27, starting transfers between devices, shift(): return lax.ppermute(value, AXES, pairs)  76.1 us
    pallas_call x19, Pallas kernels, run(): pl.pallas_call(kernel, out_shape=outs, grid_spec=pltpu.PrefetchScalarGrid...  49.9 us
    ppermute x27, waiting for transfers between devices, shift(): return lax.ppermute(value, AXES, pairs)  48.9 us
    all_to_all x4, starting transfers between devices, fetch(): return lax.all_to_all(sent, 'layer', 0, 0, tiled=True)  30.7 us
    unnamed x89, local copies, waits for them, and re-layouts  30.4 us
    all_gather x1, blocking collectives, shards(): own0 = lax.all_gather(joined, 'tensor', axis=0)  15.7 us
    all_gather x1, blocking collectives, shards(): own1 = lax.all_gather(joined, 'tensor', axis=0)  13.9 us
  transfers between devices with their start and end apart: 31, of which 14 were waited for; matrix products, arithmetic and copies ran while one was open for 1% of the time, Pallas kernels for 15%

profile of v4, /device:TPU:71, one launch (start us, length us, event | category | flops | bytes accessed | tf_op | source)
XLA Modules:
  0.0 276.3 jit_solution(15658545875390761842)
XLA Ops:
  2.3 7.8 %collective-permute-start.5 = (bf16[256,256]{1,0:T(8,128)(2,1)S(1)}, bf16[256,256]{1,0:T(8,128)(2,1)S(1)}, u32[]{:S(2)}, u32[]{:S(2)}) collective-permute-start(bf16[256,256]{1,0:T(8,128)(2,1)S(1)} %get-tuple-element.111), channel_id=1, source_target_pairs={{0,0},{1,64},{2,128},{3,192},{4,4},{5,68},{6,132},{7,196},{8,8},{9... | collective-permute-start | bytes 393224 | tf_op jit(solution)/shard_map/ppermute | solution.py:50
  16.4 9.2 %all-to-all-start = ((bf16[16,256,256]{2,1,0:T(8,128)(2,1)}), bf16[16,256,256]{2,1,0:T(8,128)(2,1)S(1)}, u32[]{:S(2)}, u32[]{:S(2)}) async-start(bf16[16,256,256]{2,1,0:T(8,128)(2,1)} %broadcast_in_dim.14), calls=%async_computation | async-start | bytes 4194304 | tf_op jit(solution)/shard_map/all_to_all | solution.py:378
  27.7 4.8 %collective-permute-start.2 = (f32[2,256]{1,0:T(2,128)S(1)}, f32[2,256]{1,0:T(2,128)S(1)}, u32[]{:S(2)}, u32[]{:S(2)}) collective-permute-start(f32[2,256]{1,0:T(2,128)S(1)} %multiply_reduce_fusion), channel_id=1, source_target_pairs={{0,2},{1,3},{2,0},{3,1},{4,6},{5,7},{6,4},{7,5},{8,10},{9,11},{10,... | collective-permute-start | bytes 6152 | tf_op jit(solution)/shard_map/ppermute | solution.py:50
  35.1 4.3 %collective-permute-start.6 = (bf16[256,256]{1,0:T(8,128)(2,1)}, bf16[256,256]{1,0:T(8,128)(2,1)S(1)}, u32[]{:S(2)}, u32[]{:S(2)}) collective-permute-start(bf16[256,256]{1,0:T(8,128)(2,1)} %get-tuple-element.67), channel_id=1, source_target_pairs={{0,0},{1,64},{2,128},{3,192},{4,4},{5,68},{6,132},{7,196},{8,8},{9... | collective-permute-start | bytes 393224 | tf_op jit(solution)/shard_map/ppermute | solution.py:50
  62.9 8.6 %all-to-all-start.1 = ((bf16[16,256,256]{2,1,0:T(8,128)(2,1)}), bf16[16,256,256]{2,1,0:T(8,128)(2,1)}, u32[]{:S(2)}, u32[]{:S(2)}) async-start(bf16[16,256,256]{2,1,0:T(8,128)(2,1)} %broadcast_in_dim.15), calls=%async_computation.1 | async-start | bytes 4194304 | tf_op jit(solution)/shard_map/all_to_all | solution.py:378
  71.5 4.4 %collective-permute-start.8 = (f32[256,256]{1,0:T(8,128)}, f32[256,256]{1,0:T(8,128)S(1)}, u32[]{:S(2)}, u32[]{:S(2)}) collective-permute-start(f32[256,256]{1,0:T(8,128)} %copy-done.43), channel_id=1, source_target_pairs={{0,1},{1,2},{2,3},{3,0},{4,5},{5,6},{6,7},{7,4},{8,9},{9,10},{10,1... | collective-permute-start | bytes 786440 | tf_op jit(solution)/shard_map/ppermute | solution.py:50
  80.1 5.0 %collective-permute-done.8.refs_1_ = f32[256,256]{1,0:T(8,128)S(1)} collective-permute-done((f32[256,256]{1,0:T(8,128)}, f32[256,256]{1,0:T(8,128)S(1)}, u32[]{:S(2)}, u32[]{:S(2)}) %collective-permute-start.8) | collective-permute-done | bytes 262176 | tf_op jit(solution)/shard_map/ppermute | solution.py:50
  85.9 14.8 %collective-permute-done.9.refs_2_ = f32[256,256]{1,0:T(8,128)S(1)} collective-permute-done((f32[256,256]{1,0:T(8,128)}, f32[256,256]{1,0:T(8,128)S(1)}, u32[]{:S(2)}, u32[]{:S(2)}) %collective-permute-start.9) | collective-permute-done | bytes 262176 | tf_op jit(solution)/shard_map/ppermute | solution.py:50
  103.9 3.6 %shard_map.82 = f32[4,256,256]{2,1,0:T(8,128)S(1)} custom-call(s32[5]{0:T(128)S(1)} %stack.23.where, bf16[2,2,4,256,256]{4,3,2,1,0:T(8,128)(2,1)S(1)} %copy-done.2, bf16[4,4,256,256]{3,2,1,0:T(8,128)(2,1)} %bitcast.10.blocks), custom_call_target="tpu_custom_call" | custom-call | flops 537000000 | bytes 6291456 | tf_op jit(solution)/shard_map/pallas_call | solution.py:212
  109.1 3.6 %shard_map.81.own = f32[4,256,256]{2,1,0:T(8,128)S(1)} custom-call(s32[5]{0:T(128)S(1)} %stack.23.where, bf16[2,2,4,256,256]{4,3,2,1,0:T(8,128)(2,1)S(1)} %copy-done.2, bf16[4,4,256,256]{3,2,1,0:T(8,128)(2,1)} %bitcast.10.blocks), custom_call_target="tpu_custom_call" | custom-call | flops 537000000 | bytes 6291456 | tf_op jit(solution)/shard_map/pallas_call | solution.py:212
  121.1 5.6 %shard_map.80 = (bf16[2,256,1024]{2,1,0:T(8,128)(2,1)}, bf16[2,256,1024]{2,1,0:T(8,128)(2,1)}, bf16[272,256]{1,0:T(8,128)(2,1)S(1)}) custom-call(f32[256,256]{1,0:T(8,128)S(1)} %copy-done.26, f32[256,256]{1,0:T(8,128)S(1)} %copy-done.28, f32[256,256]{1,0:T(8,128)S(1)} %copy-done.32, f32[256,256]{1,0:T(8,128)S(1)} %copy-done.36, ...), custom_call_target="tpu_custom_call" | custom-call | flops 5000000000 | bytes 6291456 | tf_op jit(solution)/shard_map/pallas_call | solution.py:212
  126.8 15.6 %collective-permute-done.13.refs_2_ = f32[256,256]{1,0:T(8,128)S(1)} collective-permute-done((f32[256,256]{1,0:T(8,128)S(1)}, f32[256,256]{1,0:T(8,128)S(1)}, u32[]{:S(2)}, u32[]{:S(2)}) %collective-permute-start.13) | collective-permute-done | bytes 262176 | tf_op jit(solution)/shard_map/ppermute | solution.py:50
  143.4 15.7 %all-gather = bf16[1088,256]{1,0:T(8,128)(2,1)S(1)} all-gather(bf16[272,256]{1,0:T(8,128)(2,1)S(1)} %get-tuple-element.84), channel_id=2, replica_groups=mesh['layer'=16,'dp'=4,'tensor'=4] {'tensor'}, dimensions={0}, use_global_device_ids=true | all-gather | bytes 696320 | tf_op jit(solution)/shard_map/all_gather | solution.py:405
  159.2 4.6 %collective-permute-start.15 = (bf16[4,272,256]{2,1,0:T(8,128)(2,1)S(1)}, bf16[4,272,256]{2,1,0:T(8,128)(2,1)S(1)}, u32[]{:S(2)}, u32[]{:S(2)}) collective-permute-start(bf16[4,272,256]{2,1,0:T(8,128)(2,1)S(1)} %bitcast.18), channel_id=1, source_target_pairs={{0,4},{1,5},{2,6},{3,7},{4,0},{5,1},{6,2},{7,3},{8,12},{9,13},{10,... | collective-permute-start | bytes 1671176 | tf_op jit(solution)/shard_map/ppermute | solution.py:50
  170.7 6.7 %all-to-all-start.2 = ((bf16[16,256,256]{2,1,0:T(8,128)(2,1)}), bf16[16,256,256]{2,1,0:T(8,128)(2,1)}, u32[]{:S(2)}, u32[]{:S(2)}) async-start(bf16[16,256,256]{2,1,0:T(8,128)(2,1)} %copy-done.9), calls=%async_computation.2 | async-start | bytes 4194304 | tf_op jit(solution)/shard_map/all_to_all | solution.py:378
  183.6 5.6 %shard_map.85 = (bf16[2,256,1024]{2,1,0:T(8,128)(2,1)}, bf16[2,256,1024]{2,1,0:T(8,128)(2,1)}, bf16[272,256]{1,0:T(8,128)(2,1)S(1)}) custom-call(f32[256,256]{1,0:T(8,128)S(1)} %copy-done.30, f32[256,256]{1,0:T(8,128)S(1)} %copy-done.34, f32[256,256]{1,0:T(8,128)S(1)} %copy-done.38, ...), custom_call_target="tpu_custom_call", output_to_operand_aliasing={{0}: (6, {}), {1}: (7, {})} | custom-call | flops 5000000000 | bytes 6291456 | tf_op jit(solution)/shard_map/pallas_call | solution.py:212
  189.3 13.9 %all-gather.1 = bf16[1088,256]{1,0:T(8,128)(2,1)S(1)} all-gather(bf16[272,256]{1,0:T(8,128)(2,1)S(1)} %get-tuple-element.98), channel_id=3, replica_groups=mesh['layer'=16,'dp'=4,'tensor'=4] {'tensor'}, dimensions={0}, use_global_device_ids=true | all-gather | bytes 696320 | tf_op jit(solution)/shard_map/all_gather | solution.py:413
  203.1 5.7 %collective-permute-start.16 = (bf16[4,272,256]{2,1,0:T(8,128)(2,1)S(1)}, bf16[4,272,256]{2,1,0:T(8,128)(2,1)S(1)}, u32[]{:S(2)}, u32[]{:S(2)}) collective-permute-start(bf16[4,272,256]{2,1,0:T(8,128)(2,1)S(1)} %bitcast.21), channel_id=1, source_target_pairs={{0,4},{1,5},{2,6},{3,7},{4,0},{5,1},{6,2},{7,3},{8,12},{9,13},{10,... | collective-permute-start | bytes 1671176 | tf_op jit(solution)/shard_map/ppermute | solution.py:50
  215.8 6.3 %all-to-all-start.3 = ((bf16[16,256,256]{2,1,0:T(8,128)(2,1)}), bf16[16,256,256]{2,1,0:T(8,128)(2,1)}, u32[]{:S(2)}, u32[]{:S(2)}) async-start(bf16[16,256,256]{2,1,0:T(8,128)(2,1)} %copy-done.8), calls=%async_computation.3 | async-start | bytes 4194304 | tf_op jit(solution)/shard_map/all_to_all | solution.py:378
  225.2 4.5 %shard_map.88 = (bf16[4,256,256]{2,1,0:T(8,128)(2,1)S(1)}, bf16[4,256,256]{2,1,0:T(8,128)(2,1)S(1)}) custom-call(s32[5]{0:T(128)S(1)} %constant_dynamic-update-slice_fusion.where, bf16[2,4,256,256]{3,2,1,0:T(8,128)(2,1)S(1)} %get-tuple-element.63.keep, bf16[2,4,256,256]{3,2,1,0:T(8,128)(2,1)} %collective-permute-done.sib, f32[2,256,1]{2,1,0:T(8,128)S(1)} %copy.17.inverse, ...), custom_call_target="tpu_custom_call" | custom-call | flops 1074000000 | bytes 6291456 | tf_op jit(solution)/shard_map/pallas_call | solution.py:212
  230.9 4.9 %shard_map.87 = (bf16[4,256,256]{2,1,0:T(8,128)(2,1)S(1)}, bf16[4,256,256]{2,1,0:T(8,128)(2,1)S(1)}) custom-call(s32[5]{0:T(128)S(1)} %constant_dynamic-update-slice_fusion.where, bf16[2,4,256,256]{3,2,1,0:T(8,128)(2,1)S(1)} %get-tuple-element.63.keep, bf16[2,4,256,256]{3,2,1,0:T(8,128)(2,1)} %collective-permute-done.sib, f32[2,256,1]{2,1,0:T(8,128)S(1)} %copy.17.inverse, ...), custom_call_target="tpu_custom_call" | custom-call | flops 1074000000 | bytes 6291456 | tf_op jit(solution)/shard_map/pallas_call | solution.py:212
  238.4 4.9 %collective-permute-start.19 = (bf16[256,256]{1,0:T(8,128)(2,1)S(1)}, bf16[256,256]{1,0:T(8,128)(2,1)S(1)}, u32[]{:S(2)}, u32[]{:S(2)}) collective-permute-start(bf16[256,256]{1,0:T(8,128)(2,1)S(1)} %shard_map.91), channel_id=1, source_target_pairs={{0,0},{1,64},{2,128},{3,192},{4,4},{5,68},{6,132},{7,196},{8,8},{9... | collective-permute-start | bytes 393224 | tf_op jit(solution)/shard_map/ppermute | solution.py:50
  251.1 4.7 %collective-permute-start.23 = (bf16[256,256]{1,0:T(8,128)(2,1)S(1)}, bf16[256,256]{1,0:T(8,128)(2,1)S(1)}, u32[]{:S(2)}, u32[]{:S(2)}) collective-permute-start(bf16[256,256]{1,0:T(8,128)(2,1)S(1)} %shard_map.92), channel_id=1, source_target_pairs={{0,0},{1,64},{2,128},{3,192},{4,4},{5,68},{6,132},{7,196},{8,8},{9... | collective-permute-start | bytes 393224 | tf_op jit(solution)/shard_map/ppermute | solution.py:50
  269.6 5.1 %collective-permute-done.25.refs_6_ = bf16[256,256]{1,0:T(8,128)(2,1)S(1)} collective-permute-done((bf16[256,256]{1,0:T(8,128)(2,1)S(1)}, bf16[256,256]{1,0:T(8,128)(2,1)S(1)}, u32[]{:S(2)}, u32[]{:S(2)}) %collective-permute-start.25) | collective-permute-done | bytes 131104 | tf_op jit(solution)/shard_map/ppermute | solution.py:50
  (157 shorter events, 105.3 us)
Async XLA Ops:
  2.3 12.6 %collective-permute-start.5 = (bf16[256,256]{1,0:T(8,128)(2,1)S(1)}, bf16[256,256]{1,0:T(8,128)(2,1)S(1)}, u32[]{:S(2)}, u32[]{:S(2)}) collective-permute-start(bf16[256,256]{1,0:T(8,128)(2,1)S(1)} %get-tuple-element.111), channel_id=1, source_target_pairs={{0,0},{1,64},{2,128},{3,192},{4,4},{5,68},{6,132},{7,196},{8,8},{9... | collective-permute-start | bytes 393224 | tf_op jit(solution)/shard_map/ppermute | solution.py:50
  16.4 33.8 %all-to-all-start = ((bf16[16,256,256]{2,1,0:T(8,128)(2,1)}), bf16[16,256,256]{2,1,0:T(8,128)(2,1)S(1)}, u32[]{:S(2)}, u32[]{:S(2)}) async-start(bf16[16,256,256]{2,1,0:T(8,128)(2,1)} %broadcast_in_dim.14), calls=%async_computation | async-start | bytes 4194304 | tf_op jit(solution)/shard_map/all_to_all | solution.py:378
  25.5 16.9 %collective-permute-start = (bf16[2,4,256,256]{3,2,1,0:T(8,128)(2,1)}, bf16[2,4,256,256]{3,2,1,0:T(8,128)(2,1)}, u32[]{:S(2)}, u32[]{:S(2)}) collective-permute-start(bf16[2,4,256,256]{3,2,1,0:T(8,128)(2,1)} %copy-done.24), channel_id=1, source_target_pairs={{0,4},{1,5},{2,6},{3,7},{4,0},{5,1},{6,2},{7,3},{8,12},{9,13},{10,... | collective-permute-start | bytes 3145736 | tf_op jit(solution)/shard_map/ppermute | solution.py:50
  27.7 11.8 %collective-permute-start.3 = (f32[2,256]{1,0:T(2,128)S(1)}, f32[2,256]{1,0:T(2,128)S(1)}, u32[]{:S(2)}, u32[]{:S(2)}) collective-permute-start(f32[2,256]{1,0:T(2,128)S(1)} %multiply_reduce_fusion), channel_id=1, source_target_pairs={{0,3},{1,0},{2,1},{3,2},{4,7},{5,4},{6,5},{7,6},{8,11},{9,8},{10,9... | collective-permute-start | bytes 6152 | tf_op jit(solution)/shard_map/ppermute | solution.py:50
  27.7 11.8 %collective-permute-start.2 = (f32[2,256]{1,0:T(2,128)S(1)}, f32[2,256]{1,0:T(2,128)S(1)}, u32[]{:S(2)}, u32[]{:S(2)}) collective-permute-start(f32[2,256]{1,0:T(2,128)S(1)} %multiply_reduce_fusion), channel_id=1, source_target_pairs={{0,2},{1,3},{2,0},{3,1},{4,6},{5,7},{6,4},{7,5},{8,10},{9,11},{10,... | collective-permute-start | bytes 6152 | tf_op jit(solution)/shard_map/ppermute | solution.py:50
  35.1 13.8 %collective-permute-start.6 = (bf16[256,256]{1,0:T(8,128)(2,1)}, bf16[256,256]{1,0:T(8,128)(2,1)S(1)}, u32[]{:S(2)}, u32[]{:S(2)}) collective-permute-start(bf16[256,256]{1,0:T(8,128)(2,1)} %get-tuple-element.67), channel_id=1, source_target_pairs={{0,0},{1,64},{2,128},{3,192},{4,4},{5,68},{6,132},{7,196},{8,8},{9... | collective-permute-start | bytes 393224 | tf_op jit(solution)/shard_map/ppermute | solution.py:50
  62.9 39.4 %all-to-all-start.1 = ((bf16[16,256,256]{2,1,0:T(8,128)(2,1)}), bf16[16,256,256]{2,1,0:T(8,128)(2,1)}, u32[]{:S(2)}, u32[]{:S(2)}) async-start(bf16[16,256,256]{2,1,0:T(8,128)(2,1)} %broadcast_in_dim.15), calls=%async_computation.1 | async-start | bytes 4194304 | tf_op jit(solution)/shard_map/all_to_all | solution.py:378
  71.5 13.7 %collective-permute-start.8 = (f32[256,256]{1,0:T(8,128)}, f32[256,256]{1,0:T(8,128)S(1)}, u32[]{:S(2)}, u32[]{:S(2)}) collective-permute-start(f32[256,256]{1,0:T(8,128)} %copy-done.43), channel_id=1, source_target_pairs={{0,1},{1,2},{2,3},{3,0},{4,5},{5,6},{6,7},{7,4},{8,9},{9,10},{10,1... | collective-permute-start | bytes 786440 | tf_op jit(solution)/shard_map/ppermute | solution.py:50
  76.0 24.7 %collective-permute-start.9 = (f32[256,256]{1,0:T(8,128)}, f32[256,256]{1,0:T(8,128)S(1)}, u32[]{:S(2)}, u32[]{:S(2)}) collective-permute-start(f32[256,256]{1,0:T(8,128)} %copy-done.42), channel_id=1, source_target_pairs={{0,2},{1,3},{2,0},{3,1},{4,6},{5,7},{6,4},{7,5},{8,10},{9,11},{10,... | collective-permute-start | bytes 786440 | tf_op jit(solution)/shard_map/ppermute | solution.py:50
  77.9 23.7 %collective-permute-start.10 = (f32[256,256]{1,0:T(8,128)}, f32[256,256]{1,0:T(8,128)S(1)}, u32[]{:S(2)}, u32[]{:S(2)}) collective-permute-start(f32[256,256]{1,0:T(8,128)} %copy-done.41), channel_id=1, source_target_pairs={{0,3},{1,0},{2,1},{3,2},{4,7},{5,4},{6,5},{7,6},{8,11},{9,8},{10,9... | collective-permute-start | bytes 786440 | tf_op jit(solution)/shard_map/ppermute | solution.py:50
  113.6 13.2 %collective-permute-start.12 = (f32[256,256]{1,0:T(8,128)S(1)}, f32[256,256]{1,0:T(8,128)S(1)}, u32[]{:S(2)}, u32[]{:S(2)}) collective-permute-start(f32[256,256]{1,0:T(8,128)S(1)} %get-tuple-element.81), channel_id=1, source_target_pairs={{0,1},{1,2},{2,3},{3,0},{4,5},{5,6},{6,7},{7,4},{8,9},{9,10},{10,1... | collective-permute-start | bytes 786440 | tf_op jit(solution)/shard_map/ppermute | solution.py:50
  116.5 25.9 %collective-permute-start.13 = (f32[256,256]{1,0:T(8,128)S(1)}, f32[256,256]{1,0:T(8,128)S(1)}, u32[]{:S(2)}, u32[]{:S(2)}) collective-permute-start(f32[256,256]{1,0:T(8,128)S(1)} %get-tuple-element.82), channel_id=1, source_target_pairs={{0,2},{1,3},{2,0},{3,1},{4,6},{5,7},{6,4},{7,5},{8,10},{9,11},{10,... | collective-permute-start | bytes 786440 | tf_op jit(solution)/shard_map/ppermute | solution.py:50
  119.0 23.7 %collective-permute-start.14 = (f32[256,256]{1,0:T(8,128)S(1)}, f32[256,256]{1,0:T(8,128)S(1)}, u32[]{:S(2)}, u32[]{:S(2)}) collective-permute-start(f32[256,256]{1,0:T(8,128)S(1)} %get-tuple-element.83), channel_id=1, source_target_pairs={{0,3},{1,0},{2,1},{3,2},{4,7},{5,4},{6,5},{7,6},{8,11},{9,8},{10,9... | collective-permute-start | bytes 786440 | tf_op jit(solution)/shard_map/ppermute | solution.py:50
  170.7 45.1 %all-to-all-start.2 = ((bf16[16,256,256]{2,1,0:T(8,128)(2,1)}), bf16[16,256,256]{2,1,0:T(8,128)(2,1)}, u32[]{:S(2)}, u32[]{:S(2)}) async-start(bf16[16,256,256]{2,1,0:T(8,128)(2,1)} %copy-done.9), calls=%async_computation.2 | async-start | bytes 4194304 | tf_op jit(solution)/shard_map/all_to_all | solution.py:378
  203.1 7.3 %collective-permute-start.16 = (bf16[4,272,256]{2,1,0:T(8,128)(2,1)S(1)}, bf16[4,272,256]{2,1,0:T(8,128)(2,1)S(1)}, u32[]{:S(2)}, u32[]{:S(2)}) collective-permute-start(bf16[4,272,256]{2,1,0:T(8,128)(2,1)S(1)} %bitcast.21), channel_id=1, source_target_pairs={{0,4},{1,5},{2,6},{3,7},{4,0},{5,1},{6,2},{7,3},{8,12},{9,13},{10,... | collective-permute-start | bytes 1671176 | tf_op jit(solution)/shard_map/ppermute | solution.py:50
  215.8 32.8 %all-to-all-start.3 = ((bf16[16,256,256]{2,1,0:T(8,128)(2,1)}), bf16[16,256,256]{2,1,0:T(8,128)(2,1)}, u32[]{:S(2)}, u32[]{:S(2)}) async-start(bf16[16,256,256]{2,1,0:T(8,128)(2,1)} %copy-done.8), calls=%async_computation.3 | async-start | bytes 4194304 | tf_op jit(solution)/shard_map/all_to_all | solution.py:378
  229.7 13.6 %collective-permute-start.18 = (bf16[4,256,256]{2,1,0:T(8,128)(2,1)S(1)}, bf16[4,256,256]{2,1,0:T(8,128)(2,1)S(1)}, u32[]{:S(2)}, u32[]{:S(2)}) collective-permute-start(bf16[4,256,256]{2,1,0:T(8,128)(2,1)S(1)} %get-tuple-element.107), channel_id=1, source_target_pairs={{0,4},{1,5},{2,6},{3,7},{4,0},{5,1},{6,2},{7,3},{8,12},{9,13},{10,... | collective-permute-start | bytes 1572872 | tf_op jit(solution)/shard_map/ppermute | solution.py:50
  235.8 9.2 %collective-permute-start.17 = (bf16[4,256,256]{2,1,0:T(8,128)(2,1)S(1)}, bf16[4,256,256]{2,1,0:T(8,128)(2,1)S(1)}, u32[]{:S(2)}, u32[]{:S(2)}) collective-permute-start(bf16[4,256,256]{2,1,0:T(8,128)(2,1)S(1)} %get-tuple-element.103), channel_id=1, source_target_pairs={{0,4},{1,5},{2,6},{3,7},{4,0},{5,1},{6,2},{7,3},{8,12},{9,13},{10,... | collective-permute-start | bytes 1572872 | tf_op jit(solution)/shard_map/ppermute | solution.py:50
  238.4 17.4 %collective-permute-start.19 = (bf16[256,256]{1,0:T(8,128)(2,1)S(1)}, bf16[256,256]{1,0:T(8,128)(2,1)S(1)}, u32[]{:S(2)}, u32[]{:S(2)}) collective-permute-start(bf16[256,256]{1,0:T(8,128)(2,1)S(1)} %shard_map.91), channel_id=1, source_target_pairs={{0,0},{1,64},{2,128},{3,192},{4,4},{5,68},{6,132},{7,196},{8,8},{9... | collective-permute-start | bytes 393224 | tf_op jit(solution)/shard_map/ppermute | solution.py:50
  251.1 12.1 %collective-permute-start.23 = (bf16[256,256]{1,0:T(8,128)(2,1)S(1)}, bf16[256,256]{1,0:T(8,128)(2,1)S(1)}, u32[]{:S(2)}, u32[]{:S(2)}) collective-permute-start(bf16[256,256]{1,0:T(8,128)(2,1)S(1)} %shard_map.92), channel_id=1, source_target_pairs={{0,0},{1,64},{2,128},{3,192},{4,4},{5,68},{6,132},{7,196},{8,8},{9... | collective-permute-start | bytes 393224 | tf_op jit(solution)/shard_map/ppermute | solution.py:50
  255.8 13.8 %collective-permute-start.22 = (bf16[256,256]{1,0:T(8,128)(2,1)S(1)}, bf16[256,256]{1,0:T(8,128)(2,1)S(1)}, u32[]{:S(2)}, u32[]{:S(2)}) collective-permute-start(bf16[256,256]{1,0:T(8,128)(2,1)S(1)} %collective-permute-done.19.refs_0_), channel_id=1, source_target_pairs={{0,12},{1,13},{2,14},{3,15},{4,8},{5,9},{6,10},{7,11},{8,4},{9,5},... | collective-permute-start | bytes 393224 | tf_op jit(solution)/shard_map/ppermute | solution.py:50
  258.0 11.6 %collective-permute-start.21 = (bf16[256,256]{1,0:T(8,128)(2,1)S(1)}, bf16[256,256]{1,0:T(8,128)(2,1)S(1)}, u32[]{:S(2)}, u32[]{:S(2)}) collective-permute-start(bf16[256,256]{1,0:T(8,128)(2,1)S(1)} %collective-permute-done.19.refs_0_), channel_id=1, source_target_pairs={{0,8},{1,9},{2,10},{3,11},{4,12},{5,13},{6,14},{7,15},{8,0},{9,1},... | collective-permute-start | bytes 393224 | tf_op jit(solution)/shard_map/ppermute | solution.py:50
  260.2 9.4 %collective-permute-start.20 = (bf16[256,256]{1,0:T(8,128)(2,1)S(1)}, bf16[256,256]{1,0:T(8,128)(2,1)S(1)}, u32[]{:S(2)}, u32[]{:S(2)}) collective-permute-start(bf16[256,256]{1,0:T(8,128)(2,1)S(1)} %collective-permute-done.19.refs_0_), channel_id=1, source_target_pairs={{0,4},{1,5},{2,6},{3,7},{4,0},{5,1},{6,2},{7,3},{8,12},{9,13},{10,... | collective-permute-start | bytes 393224 | tf_op jit(solution)/shard_map/ppermute | solution.py:50
  266.4 8.3 %collective-permute-start.25 = (bf16[256,256]{1,0:T(8,128)(2,1)S(1)}, bf16[256,256]{1,0:T(8,128)(2,1)S(1)}, u32[]{:S(2)}, u32[]{:S(2)}) collective-permute-start(bf16[256,256]{1,0:T(8,128)(2,1)S(1)} %collective-permute-done.23.refs_4_), channel_id=1, source_target_pairs={{0,8},{1,9},{2,10},{3,11},{4,12},{5,13},{6,14},{7,15},{8,0},{9,1},... | collective-permute-start | bytes 393224 | tf_op jit(solution)/shard_map/ppermute | solution.py:50
  (51 other events, 282.2 us)
